TPU v7x, 32 devices: a whole 2x2x4 slice. The times are simulated.
32 devices in a mesh: groups: 2 (over y), ctx: 8 (over z, x), head: 2 (over core).
Axes of the slice: x: 2, y: 2, z: 4, core: 2. Of those that a mesh axis runs over, the one named last changes fastest.
Arguments:
- queries: bfloat16 [2048, 2048], P(('groups', 'ctx'), 'head'), parts along dimension 0, may hold values from -80 to 80
- keys: bfloat16 [2048, 512], P(('groups', 'ctx'), 'head'), parts along dimension 0, may hold values from -6 to 6
- values: bfloat16 [2048, 512], P(('groups', 'ctx'), 'head'), parts along dimension 0, may hold values from -6 to 6
- pattern: int32 [16, 8], P(('groups', 'ctx')), parts along dimension 0, may hold values from -1 to 7, as said below
- x_in: bfloat16 [2048, 1024], P(('groups', 'ctx'), 'head'), parts along dimension 0, may hold values from -2 to 2
- z_gate: bfloat16 [2048, 1024], P(('groups', 'ctx'), 'head'), parts along dimension 0, may hold values from -6 to 6
- bmat: bfloat16 [2048, 256], P(('groups', 'ctx'), 'head'), parts along dimension 0, may hold values from -6 to 6
- cmat: bfloat16 [2048, 256], P(('groups', 'ctx'), 'head'), parts along dimension 0, may hold values from -0.5 to 0.5
- log_decay: float32 [32, 1024], P(('groups', 'head'), 'ctx'), parts along dimension 0, may hold values from -2 to 0
- gain: float32 [1024], P('head'), may hold values from 0.1 to 1.9
Outputs:
- attn_out: bfloat16 [2048, 2048], P(('groups', 'ctx'), 'head'), parts along dimension 0
- ssm_out: bfloat16 [2048, 1024], P(('groups', 'ctx'), 'head'), parts along dimension 0
There are 2 independent parts, one for each index of `groups`. A program takes and returns all parts, laid end to end along the dimension named above; an argument that names none is the same for every part. Nothing has to cross between parts.
Inputs may be any that keep to these rules, and one draw needn't show every extreme that they name: `pattern`: entry 0 of row q is q; the other entries are distinct blocks from q - 3 to q - 1, or -1 where no block is listed.
All inputs are finite; a program needn't handle non-finite values.
Results may differ from a plain program's by a relative error of at most 0.009.
Values may be sent and summed in bfloat16 or wider, within the bound.
A program may use at most 128 MiB of HBM per device.

v0:
```python
import jax
import jax.numpy as jnp
from jax import lax
from jax.sharding import PartitionSpec as P

BLK = 128
SCAN_BLK = 128
HD = 128
P_SIZE = 64
N = 128
KSEL = 8
REACH = 3


def entering(shard, axis, combine, identity):
    peers, index = (lax.axis_size(axis), lax.axis_index(axis))
    everything = jax.tree.map(lambda part: lax.all_gather(part, axis), shard)
    start = jax.tree.map(
        lambda part, zero: jnp.broadcast_to(jnp.asarray(zero, part.dtype), part.shape),
        shard,
        identity,
    )

    def step(k, before):
        reached = k < index
        new = combine(before, jax.tree.map(lambda part: part[k], everything))
        return jax.tree.map(lambda a, b: jnp.where(reached, a, b), new, before)

    return lax.fori_loop(0, peers, step, start)


def passed_along(value, axis, steps):
    count = lax.axis_size(axis)
    initial, last = (max(0, -steps), min(count, count - steps))
    return lax.ppermute(value, axis, [(source, source + steps) for source in range(initial, last)])


def combine_states(earlier, later):
    return (earlier[0] + later[0], jnp.exp(later[0])[..., None, None] * earlier[1] + later[1])


def split_parts(multiplier):
    upper = multiplier.astype(jnp.bfloat16)
    lower = (multiplier - upper.astype(jnp.float32)).astype(jnp.bfloat16)
    return (upper, lower)


def two_pass(form, multiplier, other):
    upper, lower = split_parts(multiplier)
    first = jnp.einsum(form, upper, other, preferred_element_type=jnp.float32)
    return first + jnp.einsum(form, lower, other, preferred_element_type=jnp.float32)


def double_sweep_right(form, other, multiplier):
    upper, lower = split_parts(multiplier)
    first = jnp.einsum(form, other, upper, preferred_element_type=jnp.float32)
    return first + jnp.einsum(form, other, lower, preferred_element_type=jnp.float32)


def mamba_mixer(x_in, z_gate, bmat, cmat, log_decay, gain, length):
    total_len = x_in.shape[0]
    heads_here = log_decay.shape[0]
    groups_here = bmat.shape[1] // N
    per_group = heads_here // groups_here
    block_count = total_len // length
    x_half = x_in.reshape(block_count, length, groups_here, per_group, P_SIZE)
    b_half = bmat.reshape(block_count, length, groups_here, N)
    c_half = cmat.reshape(block_count, length, groups_here, N)
    log_rates = log_decay.reshape(groups_here, per_group, block_count, length)
    cumulative = jnp.cumsum(log_rates, axis=3)
    spread = cumulative[..., :, None] - cumulative[..., None, :]
    lower_tri = jnp.tril(jnp.ones((length, length), dtype=bool))
    decays = jnp.exp(jnp.where(lower_tri, spread, -jnp.inf))
    affinity = jnp.einsum("clgn,cmgn->cglm", c_half, b_half, preferred_element_type=jnp.float32)
    mixing = affinity[:, :, None] * jnp.transpose(decays, (2, 0, 1, 3, 4))
    inside = two_pass("cghlm,cmghp->clghp", mixing, x_half)
    weights = jnp.exp(cumulative[..., -1:] - cumulative)
    weighted = x_half.astype(jnp.float32) * jnp.transpose(weights, (2, 3, 0, 1))[..., None]
    summary = two_pass("clghp,clgn->cghpn", weighted, b_half)
    block_decay = cumulative[..., -1]
    running = jnp.zeros((groups_here, per_group, P_SIZE, N), jnp.float32)
    decay_sum = jnp.zeros((groups_here, per_group), jnp.float32)
    starts = running
    prefixes = decay_sum
    running = jnp.exp(block_decay[..., 0])[..., None, None] * running + summary[0]
    decay_sum = block_decay[..., 0]
    identity = (jnp.zeros_like(decay_sum), jnp.zeros_like(running))
    incoming = entering((decay_sum, running), "ctx", combine_states, identity)
    entry = jnp.stack([starts + jnp.exp(prefixes)[..., None, None] * incoming[1]])
    carried = double_sweep_right("clgn,cghpn->clghp", c_half, entry)
    carried = carried * jnp.transpose(jnp.exp(cumulative), (2, 3, 0, 1))[..., None]
    mixed_rows = (inside + carried).reshape(total_len, heads_here * P_SIZE)
    gated_rows = mixed_rows * jax.nn.silu(z_gate.astype(jnp.float32))
    grouped = gated_rows.reshape(total_len, groups_here, per_group * P_SIZE)
    inverse_rms = lax.rsqrt(jnp.mean(grouped * grouped, axis=-1, keepdims=True) + 1e-05)
    scaled = grouped * inverse_rms * gain.reshape(groups_here, per_group * P_SIZE)
    return scaled.reshape(total_len, heads_here * P_SIZE).astype(jnp.bfloat16)


def attention_local(queries, keys, values, pattern):
    total_len = queries.shape[0]
    per_shard = total_len // BLK
    kv_heads = keys.shape[1] // HD
    members = queries.shape[1] // keys.shape[1]
    position = lax.axis_index("ctx")
    stacked = jnp.stack([keys, values])
    window = stacked
    span_now = 1
    while span_now <= REACH:
        arrived = passed_along(window, "ctx", span_now)
        window = jnp.concatenate([arrived, window], axis=1)
        span_now = span_now * 2
    window_blocks = window.reshape(2, -1, BLK, kv_heads, HD)
    first_block = (position - REACH) * per_shard
    local_index = jnp.clip(pattern - first_block, 0, window_blocks.shape[1] - 1)
    key_sel = window_blocks[0][local_index].reshape(per_shard, KSEL * BLK, kv_heads, HD)
    value_sel = window_blocks[1][local_index].reshape(per_shard, KSEL * BLK, kv_heads, HD)
    q_rows = queries.reshape(per_shard, BLK, kv_heads, members, HD)
    scores = jnp.einsum(
        "bqkgd,bmkd->bkgqm", q_rows, key_sel, preferred_element_type=jnp.float32
    ) * HD ** (-0.5)
    key_pos = (pattern[:, :, None] * BLK + jnp.arange(BLK, dtype=jnp.int32)[None, None, :]).reshape(
        per_shard, KSEL * BLK
    )
    query_pos = (position * per_shard + jnp.arange(per_shard, dtype=jnp.int32))[
        :, None
    ] * BLK + jnp.arange(BLK, dtype=jnp.int32)[None, :]
    usable = jnp.repeat(pattern >= 0, BLK, axis=1)
    allowed = usable[:, None, :] & (key_pos[:, None, :] <= query_pos[:, :, None])
    scores = jnp.where(allowed[:, None, None], scores, -jnp.inf)
    row_max = jnp.max(scores, axis=-1, keepdims=True)
    expo = jnp.exp(scores - row_max)
    row_total = jnp.sum(expo, axis=-1)
    rounded = expo.astype(jnp.bfloat16)
    mixed_rows = jnp.einsum(
        "bkgqm,bmkd->bqkgd", rounded, value_sel, preferred_element_type=jnp.float32
    )
    mixed_rows = mixed_rows / jnp.transpose(row_total, (0, 3, 1, 2))[..., None]
    return mixed_rows.reshape(total_len, kv_heads * members * HD).astype(jnp.bfloat16)


def on_device(queries, keys, values, pattern, x_in, z_gate, bmat, cmat, log_decay, gain):
    attn_out = attention_local(queries, keys, values, pattern)
    length = SCAN_BLK
    ssm_out = mamba_mixer(x_in, z_gate, bmat, cmat, log_decay, gain, length)
    return (attn_out, ssm_out)


def solution(mesh):
    placed = (
        P(("groups", "ctx"), "head"),
        P(("groups", "ctx"), "head"),
        P(("groups", "ctx"), "head"),
        P(("groups", "ctx"), None),
        P(("groups", "ctx"), "head"),
        P(("groups", "ctx"), "head"),
        P(("groups", "ctx"), "head"),
        P(("groups", "ctx"), "head"),
        P(("groups", "head"), "ctx"),
        P("head"),
    )
    return jax.shard_map(
        on_device,
        mesh=mesh,
        in_specs=placed,
        out_specs=(P(("groups", "ctx"), "head"), P(("groups", "ctx"), "head")),
        check_vma=False,
    )
```

profile of v0, /device:TPU:0, one launch (start us, length us, event | category | flops | bytes accessed | tf_op | source)
XLA Modules:
  0.0 83.3 jit_solution(15571325007035407345)
XLA Ops:
  7.2 1.0 %reduce_window_sum.11 = f32[1,8,1,128]{3,1,2,0:T(8,128)S(1)} reduce-window(f32[1,8,1,128]{3,1,2,0:T(8,128)} %bitcast.157, f32[]{:T(128)} %constant.58.clone.1), window={size=1x1x1x128 pad=0_0x0_0x0_0x127_0}, to_apply=%region_2.3 | reduce-window | flops 130048 | bytes 8196 | tf_op jit(solution)/shard_map/jit(cumsum)/reduce_window_sum | solution.py:70
  8.4 1.0 %copy.39 = bf16[128,512]{0,1:T(8,128)(2,1)S(1)} copy(bf16[128,512]{1,0:T(8,128)(2,1)} %param.16) | data formatting | bytes 262144 | tf_op args[4]
  9.8 0.9 %fusion.12 = f32[8,64,128]{2,1,0:T(8,128)} fusion(f32[8,64,128]{2,1,0:T(8,128)S(1)} %fusion.52, bf16[128,8,64]{0,2,1:T(8,128)(2,1)S(1)} %bitcast.149, f32[8]{0:T(128)S(1)} %get-tuple-element.136, bf16[128,128]{1,0:T(8,128)(2,1)S(1)} %copy-done), kind=kOutput, calls=%fused_computation.17 | convolution fusion | flops 16908288 | bytes 688160 | tf_op jit(solution)/shard_map/clghp,clgn->cghpn/dot_general | solution.py:51
  10.7 0.9 %pad_maximum_fusion = bf16[2,128,256]{2,1,0:T(8,128)(2,1)S(1)} fusion(bf16[1,128,256]{2,1,0:T(8,128)(2,1)} %bitcast.140, bf16[1,128,256]{2,1,0:T(8,128)(2,1)} %bitcast.143), kind=kLoop, calls=%fused_computation.57 | loop fusion | flops 65536 | bytes 262144 | tf_op jit(solution)/shard_map/stack | solution.py:106
  11.6 4.9 %collective-permute-start = (bf16[2,128,256]{2,1,0:T(8,128)(2,1)S(1)}, bf16[2,128,256]{2,1,0:T(8,128)(2,1)S(1)}, u32[]{:S(2)}, u32[]{:S(2)}) collective-permute-start(bf16[2,128,256]{2,1,0:T(8,128)(2,1)S(1)} %pad_maximum_fusion), channel_id=1, source_target_pairs={{0,2},{2,4},{4,6},{6,8},{8,10},{10,12},{12,14},{1,3},{3,5},{5,7},{... | collective-permute-start | bytes 393224 | tf_op jit(solution)/shard_map/ppermute | solution.py:35
  18.3 0.9 %fusion.60 = f32[128,128]{1,0:T(8,128)S(1)} fusion(bf16[128,128]{1,0:T(8,128)(2,1)} %param.19, bf16[128,128]{1,0:T(8,128)(2,1)S(1)} %copy-done), kind=kOutput, calls=%fused_computation.86 | convolution fusion | flops 4194304 | bytes 131072 | tf_op jit(solution)/shard_map/clgn,cmgn->cglm/dot_general | solution.py:74
  19.2 0.9 %maximum_maximum_fusion.1 = bf16[2,256,256]{2,1,0:T(8,128)(2,1)S(1)} fusion(bf16[1,128,256]{2,1,0:T(8,128)(2,1)} %bitcast.141, bf16[1,128,256]{2,1,0:T(8,128)(2,1)} %bitcast.144, bf16[2,128,256]{2,1,0:T(8,128)(2,1)S(1)} %collective-permute-done), kind=kLoop, calls=%fused_computation.37 | loop fusion | flops 786432 | bytes 524288 | tf_op jit(solution)/shard_map/concatenate | solution.py:111
  20.1 5.3 %collective-permute-start.1 = (bf16[2,256,256]{2,1,0:T(8,128)(2,1)S(1)}, bf16[2,256,256]{2,1,0:T(8,128)(2,1)S(1)}, u32[]{:S(2)}, u32[]{:S(2)}) collective-permute-start(bf16[2,256,256]{2,1,0:T(8,128)(2,1)S(1)} %maximum_maximum_fusion.1), channel_id=1, source_target_pairs={{0,4},{2,6},{4,8},{6,10},{8,12},{10,14},{1,5},{3,7},{5,9},{7,11},{... | collective-permute-start | bytes 786440 | tf_op jit(solution)/shard_map/ppermute | solution.py:35
  25.5 1.1 %reshape.353 = bf16[128,2,4,128]{3,2,1,0:T(4,128)(2,1)S(1)} reshape(bf16[128,1024]{1,0:T(8,128)(2,1)} %param.12) | data formatting | bytes 524288 | tf_op jit(solution)/shard_map/reshape.25
  26.7 24.0 %all-gather = f32[8,8,1,1]{1,3,2,0:T(1,128)S(1)} all-gather(f32[1,8,1,1]{1,3,2,0:T(1,128)S(1)} %copy.40), channel_id=2, replica_groups=mesh['groups'=2,'ctx'=8,'head'=2] {'ctx'}, dimensions={0}, use_global_device_ids=true | all-gather | bytes 288 | tf_op jit(solution)/shard_map/all_gather | solution.py:17
  51.2 1.6 %gather_fusion.1 = bf16[8,128,2,128]{3,2,1,0:T(2,128)(2,1)S(1)} fusion(bf16[4,128,2,128]{3,2,1,0:T(2,128)(2,1)S(1)} %squeeze.18, s32[1024]{0:T(1024)S(1)} %pad_clamp_fusion), kind=kCustom, calls=%fused_computation.1 | custom fusion | bytes 1048608 | tf_op jit(solution)/shard_map/gather | solution.py:116
  53.0 1.6 %gather_fusion = bf16[8,128,2,128]{3,2,1,0:T(2,128)(2,1)S(1)} fusion(bf16[4,128,2,128]{3,2,1,0:T(2,128)(2,1)S(1)} %squeeze.17, s32[1024]{0:T(1024)S(1)} %pad_clamp_fusion), kind=kCustom, calls=%fused_computation | custom fusion | bytes 1048608 | tf_op jit(solution)/shard_map/gather | solution.py:117
  55.4 0.9 %fusion.1 = f32[2,4,128]{2,1,0:T(4,128)S(1)} fusion(f32[2,1024,128,4]{2,1,3,0:T(8,128)S(1)} %get-tuple-element.158, f32[2,4,128]{2,1,0:T(4,128)S(1)} %get-tuple-element.157, pred[128,1024]{0,1:T(8,128)(4,1)S(1)} %compare_and_fusion), kind=kLoop, calls=%fused_computation.7 | loop fusion | flops 4193280 | bytes 4333568 | tf_op jit(solution)/shard_map/reduce_sum | solution.py:133
  56.2 1.1 %fusion.19 = bf16[1,128,2,4,128]{1,4,3,2,0:T(8,128)(2,1)S(1)} fusion(f32[2,1024,128,4]{2,1,3,0:T(8,128)S(1)} %get-tuple-element.158, f32[2,4,128]{2,1,0:T(4,128)S(1)} %get-tuple-element.157, pred[128,1024]{0,1:T(8,128)(4,1)S(1)} %compare_and_fusion, bf16[1024,2,128,1]{2,1,0,3:T(2,128)(2,1)S(1)} %bitcast.150, f32[128,2,4]{0,2,1:T(4,128)S(1)} %bitcast.158), kind=kOutput, calls=%fused_computation.23 | convolution fusion | flops 272891904 | bytes 5120000 | tf_op jit(solution)/shard_map/bkgqm,bmkd->bqkgd/dot_general | solution.py:135
  58.2 7.6 %all-gather.4.cloned.1.call-done = f32[64,64,128]{2,1,0:T(8,128)} async-done(((f32[8,64,128]{2,1,0:T(8,128)}), f32[64,64,128]{2,1,0:T(8,128)}) %all-gather.4.cloned.1.call-update) | async-done | bytes 2097168 | tf_op jit(solution)/shard_map/all_gather | solution.py:17
  65.9 8.7 %while.14 = (s32[]{:T(128)}, f32[1,8,64,128]{3,2,1,0:T(8,128)S(1)}, s32[]{:T(128)}, f32[8,1,8]{2,1,0:T(1,128)S(1)}, f32[8,1,8,64,128]{4,3,2,1,0:T(8,128)}, /*index=5*/s32[]{:T(128)}, s32[]{:T(128)}) while((s32[]{:T(128)}, f32[1,8,64,128]{3,2,1,0:T(8,128)S(1)}, s32[]{:T(128)}, f32[8,1,8]{2,1,0:T(1,128)S(1)}, ...), condition=%wide.region_4.5_spmd.clone, body=%wide.region_3.4_spmd.clone.sunk | while | flops 262148 | bytes 786641 | solution.py:29
  65.9 1.1 %fusion.69 = f32[1,8,64,128]{3,2,1,0:T(8,128)S(1)} fusion(f32[8,1,8,64,128]{4,3,2,1,0:T(8,128)} %get-tuple-element.208, s32[]{:T(128)S(6)} %copy.60, f32[1,8,64,128]{3,2,1,0:T(8,128)S(1)} %get-tuple-element.198, f32[8]{0:T(128)S(1)} %exponential_bitcast_fusion.4, pred[]{:T(512)S(6)} %compare.3, pred[]{:T(512)S(6)} %lt.30), kind=kLoop, calls=%fused_computation.3.clone.1 | loop fusion | flops 262144 | bytes 786470 | tf_op jit(solution)/shard_map/while/body/eval_jaxpr/jit(_where)/select_n | solution.py:27
  67.0 1.1 %fusion.69 = f32[1,8,64,128]{3,2,1,0:T(8,128)S(1)} fusion(f32[8,1,8,64,128]{4,3,2,1,0:T(8,128)} %get-tuple-element.208, s32[]{:T(128)S(6)} %copy.60, f32[1,8,64,128]{3,2,1,0:T(8,128)S(1)} %get-tuple-element.198, f32[8]{0:T(128)S(1)} %exponential_bitcast_fusion.4, pred[]{:T(512)S(6)} %compare.3, pred[]{:T(512)S(6)} %lt.30), kind=kLoop, calls=%fused_computation.3.clone.1 | loop fusion | flops 262144 | bytes 786470 | tf_op jit(solution)/shard_map/while/body/eval_jaxpr/jit(_where)/select_n | solution.py:27
  68.1 1.1 %fusion.69 = f32[1,8,64,128]{3,2,1,0:T(8,128)S(1)} fusion(f32[8,1,8,64,128]{4,3,2,1,0:T(8,128)} %get-tuple-element.208, s32[]{:T(128)S(6)} %copy.60, f32[1,8,64,128]{3,2,1,0:T(8,128)S(1)} %get-tuple-element.198, f32[8]{0:T(128)S(1)} %exponential_bitcast_fusion.4, pred[]{:T(512)S(6)} %compare.3, pred[]{:T(512)S(6)} %lt.30), kind=kLoop, calls=%fused_computation.3.clone.1 | loop fusion | flops 262144 | bytes 786470 | tf_op jit(solution)/shard_map/while/body/eval_jaxpr/jit(_where)/select_n | solution.py:27
  69.1 1.1 %fusion.69 = f32[1,8,64,128]{3,2,1,0:T(8,128)S(1)} fusion(f32[8,1,8,64,128]{4,3,2,1,0:T(8,128)} %get-tuple-element.208, s32[]{:T(128)S(6)} %copy.60, f32[1,8,64,128]{3,2,1,0:T(8,128)S(1)} %get-tuple-element.198, f32[8]{0:T(128)S(1)} %exponential_bitcast_fusion.4, pred[]{:T(512)S(6)} %compare.3, pred[]{:T(512)S(6)} %lt.30), kind=kLoop, calls=%fused_computation.3.clone.1 | loop fusion | flops 262144 | bytes 786470 | tf_op jit(solution)/shard_map/while/body/eval_jaxpr/jit(_where)/select_n | solution.py:27
  70.2 1.1 %fusion.69 = f32[1,8,64,128]{3,2,1,0:T(8,128)S(1)} fusion(f32[8,1,8,64,128]{4,3,2,1,0:T(8,128)} %get-tuple-element.208, s32[]{:T(128)S(6)} %copy.60, f32[1,8,64,128]{3,2,1,0:T(8,128)S(1)} %get-tuple-element.198, f32[8]{0:T(128)S(1)} %exponential_bitcast_fusion.4, pred[]{:T(512)S(6)} %compare.3, pred[]{:T(512)S(6)} %lt.30), kind=kLoop, calls=%fused_computation.3.clone.1 | loop fusion | flops 262144 | bytes 786470 | tf_op jit(solution)/shard_map/while/body/eval_jaxpr/jit(_where)/select_n | solution.py:27
  71.3 1.1 %fusion.69 = f32[1,8,64,128]{3,2,1,0:T(8,128)S(1)} fusion(f32[8,1,8,64,128]{4,3,2,1,0:T(8,128)} %get-tuple-element.208, s32[]{:T(128)S(6)} %copy.60, f32[1,8,64,128]{3,2,1,0:T(8,128)S(1)} %get-tuple-element.198, f32[8]{0:T(128)S(1)} %exponential_bitcast_fusion.4, pred[]{:T(512)S(6)} %compare.3, pred[]{:T(512)S(6)} %lt.30), kind=kLoop, calls=%fused_computation.3.clone.1 | loop fusion | flops 262144 | bytes 786470 | tf_op jit(solution)/shard_map/while/body/eval_jaxpr/jit(_where)/select_n | solution.py:27
  72.4 1.1 %fusion.69 = f32[1,8,64,128]{3,2,1,0:T(8,128)S(1)} fusion(f32[8,1,8,64,128]{4,3,2,1,0:T(8,128)} %get-tuple-element.208, s32[]{:T(128)S(6)} %copy.60, f32[1,8,64,128]{3,2,1,0:T(8,128)S(1)} %get-tuple-element.198, f32[8]{0:T(128)S(1)} %exponential_bitcast_fusion.4, pred[]{:T(512)S(6)} %compare.3, pred[]{:T(512)S(6)} %lt.30), kind=kLoop, calls=%fused_computation.3.clone.1 | loop fusion | flops 262144 | bytes 786470 | tf_op jit(solution)/shard_map/while/body/eval_jaxpr/jit(_where)/select_n | solution.py:27
  73.5 1.1 %fusion.69 = f32[1,8,64,128]{3,2,1,0:T(8,128)S(1)} fusion(f32[8,1,8,64,128]{4,3,2,1,0:T(8,128)} %get-tuple-element.208, s32[]{:T(128)S(6)} %copy.60, f32[1,8,64,128]{3,2,1,0:T(8,128)S(1)} %get-tuple-element.198, f32[8]{0:T(128)S(1)} %exponential_bitcast_fusion.4, pred[]{:T(512)S(6)} %compare.3, pred[]{:T(512)S(6)} %lt.30), kind=kLoop, calls=%fused_computation.3.clone.1 | loop fusion | flops 262144 | bytes 786470 | tf_op jit(solution)/shard_map/while/body/eval_jaxpr/jit(_where)/select_n | solution.py:27
  (54 shorter events, 6.7 us)
Async XLA Ops:
  7.2 2.4 %copy-start = (bf16[128,128]{1,0:T(8,128)(2,1)S(1)}, bf16[128,128]{1,0:T(8,128)(2,1)}, u32[]{:S(2)}) copy-start(bf16[128,128]{1,0:T(8,128)(2,1)} %param.18) | copy-start | bytes 98308
  7.2 43.9 %copy-start.1 = (bf16[128,256]{1,0:T(8,128)(2,1)S(1)}, bf16[128,256]{1,0:T(8,128)(2,1)}, u32[]{:S(2)}) copy-start(bf16[128,256]{1,0:T(8,128)(2,1)} %param.14) | copy-start | bytes 196612
  7.2 43.9 %copy-start.2 = (bf16[128,256]{1,0:T(8,128)(2,1)S(1)}, bf16[128,256]{1,0:T(8,128)(2,1)}, u32[]{:S(2)}) copy-start(bf16[128,256]{1,0:T(8,128)(2,1)} %param.13) | copy-start | bytes 196612
  7.2 58.7 %all-gather.4.cloned.1.call-start = ((), (), s32[]{:S(2)}) async-start(), calls=%async_computation | async-start | bytes 2359296 | tf_op jit(solution)/shard_map/all_gather | solution.py:17
  11.6 7.6 %collective-permute-start = (bf16[2,128,256]{2,1,0:T(8,128)(2,1)S(1)}, bf16[2,128,256]{2,1,0:T(8,128)(2,1)S(1)}, u32[]{:S(2)}, u32[]{:S(2)}) collective-permute-start(bf16[2,128,256]{2,1,0:T(8,128)(2,1)S(1)} %pad_maximum_fusion), channel_id=1, source_target_pairs={{0,2},{2,4},{4,6},{6,8},{8,10},{10,12},{12,14},{1,3},{3,5},{5,7},{... | collective-permute-start | bytes 393224 | tf_op jit(solution)/shard_map/ppermute | solution.py:35
  20.1 30.9 %collective-permute-start.1 = (bf16[2,256,256]{2,1,0:T(8,128)(2,1)S(1)}, bf16[2,256,256]{2,1,0:T(8,128)(2,1)S(1)}, u32[]{:S(2)}, u32[]{:S(2)}) collective-permute-start(bf16[2,256,256]{2,1,0:T(8,128)(2,1)S(1)} %maximum_maximum_fusion.1), channel_id=1, source_target_pairs={{0,4},{2,6},{4,8},{6,10},{8,12},{10,14},{1,5},{3,7},{5,9},{7,11},{... | collective-permute-start | bytes 786440 | tf_op jit(solution)/shard_map/ppermute | solution.py:35
  57.3 17.3 %copy-start.4 = (bf16[128,128]{1,0:T(8,128)(2,1)S(1)}, bf16[128,128]{1,0:T(8,128)(2,1)}, u32[]{:S(2)}) copy-start(bf16[128,128]{1,0:T(8,128)(2,1)} %param.19) | copy-start | bytes 98308
  57.3 18.2 %copy-start.3 = (bf16[128,512]{1,0:T(8,128)(2,1)S(1)}, bf16[128,512]{1,0:T(8,128)(2,1)}, u32[]{:S(2)}) copy-start(bf16[128,512]{1,0:T(8,128)(2,1)} %param.17) | copy-start | bytes 393220
  57.4 18.3 %copy-start.5 = (f32[512]{0:T(512)S(1)}, f32[512]{0:T(512)}, u32[]{:S(2)}) copy-start(f32[512]{0:T(512)} %param.21) | copy-start | bytes 6148
Sparse Core Ops, SparseCore 0:
  10.8 54.9 all-gather.3
where the time goes:
time: 84 us; the launch traced here: 83.3 us
  blocking collectives  24 us (29%)
  other arithmetic  15.1 us (18%)
  between operations  14.3 us (17%)
  starting transfers between devices  10.2 us (12%)
  waiting for transfers between devices  7.65 us (9%)
  local copies, waits for them, and re-layouts  6.94 us (8%)
  matrix products  4.89 us (6%)
    all_gather x1, blocking collectives, entering(): everything = jax.tree.map(lambda part: lax.all_gather(part, axis), shard)  24 us
    ppermute x2, starting transfers between devices, passed_along(): lax.ppermute(value, axis, [(source, source + steps) for source in range(i...  10.2 us
    select_n x8, other arithmetic, step(): return jax.tree.map(lambda a, b: jnp.where(reached, a, b), new, before)  8.42 us
    all_gather x1, waiting for transfers between devices, entering(): everything = jax.tree.map(lambda part: lax.all_gather(part, axis), shard)  7.63 us
    unnamed x14, local copies, waits for them, and re-layouts  1.92 us
    gather x2, local copies, waits for them, and re-layouts, attention_local(): window_blocks[0][local_index].reshape(per_shard, KSEL * BLK, kv_heads, HD)  1.7 us
  transfers between devices with their start and end apart: 3, of which 1 were waited for; matrix products, arithmetic and copies ran while one was open for 16% of the time, Pallas kernels for 0%

commit v1 on v0

v1 whole, which is shorter than its diff:
```python
import functools

import jax
import jax.numpy as jnp
from jax import lax
from jax.experimental import pallas as pl
from jax.experimental.pallas import tpu as pltpu
from jax.sharding import PartitionSpec as P

BLK = 128
HD = 128
P_SIZE = 64
N = 128
UNLISTED = -1e30
EXACT = lax.Precision.HIGHEST
MESH = pl.DeviceIdType.MESH


def dot(a, b, precision=None):
    return jnp.dot(a, b, preferred_element_type=jnp.float32, precision=precision)


def dot_rows(a, b):
    return lax.dot_general(a, b, (((1,), (1,)), ((), ())), preferred_element_type=jnp.float32)


def dot_state(c, state):
    if state.dtype == jnp.bfloat16:
        return dot(c, state)
    upper = state.astype(jnp.bfloat16)
    lower = (state - upper.astype(jnp.float32)).astype(jnp.bfloat16)
    return dot(c, upper) + dot(c, lower)


def kernel(
    n, state_type,
    q_ref, k_ref, v_ref, pat_ref, x_ref, z_ref, b_ref, c_ref, ld_ref, gain_ref,
    attn_ref, ssm_ref,
    kv_own, kv_in, ld_in, s_own, s_in, p_out, p_in, y_ref, grow_ref, acc_ref, max_ref, sum_ref,
    kv_send, kv_recv, ld_send, ld_recv, s_send, s_recv, p_send, p_recv,
):
    me = lax.axis_index("ctx")
    pair = me // 2
    side = me % 2
    partner = me + 1 - 2 * side
    has_next = me + 2 < n
    has_before = me >= 2
    heads = ld_ref.shape[0]
    width = heads * P_SIZE
    chunks = width // 128
    kv_heads = k_ref.shape[1] // HD
    members = q_ref.shape[1] // k_ref.shape[1]

    barrier = pltpu.get_barrier_semaphore()
    for away in (-2, -1, 1, 2):
        @pl.when((me + away >= 0) & (me + away < n))
        def _():
            pl.semaphore_signal(barrier, inc=1, device_id={"ctx": me + away}, device_id_type=MESH)

    def copy(src, dst, send_sem, recv_sem, target):
        return pltpu.make_async_remote_copy(
            src_ref=src, dst_ref=dst, send_sem=send_sem, recv_sem=recv_sem,
            device_id={"ctx": target}, device_id_type=MESH,
        )

    def kv_copy(src, slot, which, target):
        return copy(src, kv_in.at[slot], kv_send.at[which], kv_recv.at[slot], target)

    to_next = kv_copy(kv_own, 1, 0, me + 2)
    to_pair = kv_copy(kv_own, 0, 1, me + 1)
    relay_up = kv_copy(kv_in.at[1], 2, 2, me + 1)
    relay_down = kv_copy(kv_in.at[1], 0, 3, me - 1)
    ld_copy = copy(ld_ref, ld_in, ld_send, ld_recv, partner)
    s_copies = [
        copy(s_own.at[k], s_in.at[k], s_send.at[k], s_recv.at[k], partner) for k in range(chunks)
    ]
    p_copies = [
        copy(p_out.at[k], p_in.at[k], p_send.at[k], p_recv.at[k], me + 2) for k in range(chunks)
    ]

    kv_own[0] = k_ref[...]
    kv_own[1] = v_ref[...]

    row = lax.broadcasted_iota(jnp.int32, (BLK, BLK), 0)
    col = lax.broadcasted_iota(jnp.int32, (BLK, BLK), 1)
    log_rates = ld_ref[...]
    cum_row = dot(log_rates, (row <= col).astype(jnp.float32), EXACT)
    cum_col = cum_row.T
    head_of = (
        lax.broadcasted_iota(jnp.int32, (heads, width), 1) // P_SIZE
        == lax.broadcasted_iota(jnp.int32, (heads, width), 0)
    ).astype(jnp.float32)
    cum_wide = dot(cum_col, head_of, EXACT)
    total_own = cum_wide[BLK - 1 :, :]
    weighted = (x_ref[...].astype(jnp.float32) * jnp.exp(total_own - cum_wide)).astype(jnp.bfloat16)
    b_turned = b_ref[...].astype(jnp.float32).T.astype(jnp.bfloat16)
    summary = dot(b_turned, weighted).astype(state_type)
    for k in range(chunks):
        s_own[k] = summary[:, k * 128 : (k + 1) * 128]

    @pl.when(pair == 0)
    def _():
        p_in[...] = jnp.zeros_like(p_in)

    peers = jnp.minimum(me, 2) + jnp.minimum(n - 1 - me, 2)
    pl.semaphore_wait(barrier, peers)

    ld_copy.start()
    for each in s_copies:
        each.start()

    @pl.when(has_next)
    def _():
        to_next.start()

    @pl.when(side == 0)
    def _():
        to_pair.start()

    affinity = dot_rows(c_ref[...], b_ref[...])
    for k in range(chunks):
        x_pair = x_ref[:, k * 128 : (k + 1) * 128]
        halves = []
        for h in (2 * k, 2 * k + 1):
            spread = cum_col[:, h : h + 1] - cum_row[h : h + 1, :]
            decays = jnp.exp(jnp.where(row >= col, spread, -jnp.inf))
            halves.append(dot((affinity * decays).astype(jnp.bfloat16), x_pair))
        y_ref[:, k * 128 : (k + 1) * 128] = jnp.where(col < P_SIZE, halves[0], halves[1])
    grow_ref[...] = jnp.exp(cum_wide)

    def head_rows(c):
        return jnp.concatenate(
            [q_ref[:, (c * members + j) * HD : (c * members + j + 1) * HD] for j in range(members)],
            axis=0,
        )

    def scores_of(keys, c):
        return dot_rows(keys, head_rows(c)) * HD ** (-0.5)

    def own_block():
        key_at = lax.broadcasted_iota(jnp.int32, (BLK, members * BLK), 0)
        query_at = lax.broadcasted_iota(jnp.int32, (BLK, members * BLK), 1) % BLK
        for c in range(kv_heads):
            scores = scores_of(k_ref[:, c * HD : (c + 1) * HD], c)
            scores = jnp.where(key_at <= query_at, scores, UNLISTED)
            top = jnp.max(scores, axis=0, keepdims=True)
            expo = jnp.exp(scores - top)
            v_turned = v_ref[:, c * HD : (c + 1) * HD].astype(jnp.float32).T.astype(jnp.bfloat16)
            acc_ref[c] = dot(v_turned, expo.astype(jnp.bfloat16))
            max_ref[c] = top
            sum_ref[c] = jnp.sum(expo, axis=0, keepdims=True)

    def earlier_block(slot):
        listed = jnp.max(
            jnp.where(pat_ref[...] == me - 1 - slot, 0.0, UNLISTED), axis=1, keepdims=True
        )
        for c in range(kv_heads):
            scores = scores_of(kv_in[slot, 0, :, c * HD : (c + 1) * HD], c) + listed
            before = max_ref[c]
            top = jnp.maximum(before, jnp.max(scores, axis=0, keepdims=True))
            scale = jnp.exp(before - top)
            expo = jnp.exp(scores - top)
            v_turned = (
                kv_in[slot, 1, :, c * HD : (c + 1) * HD].astype(jnp.float32).T.astype(jnp.bfloat16)
            )
            acc_ref[c] = acc_ref[c] * scale + dot(v_turned, expo.astype(jnp.bfloat16))
            max_ref[c] = top
            sum_ref[c] = sum_ref[c] * scale + jnp.sum(expo, axis=0, keepdims=True)

    def arrive_and_use(slot):
        if slot != 1:
            kv_copy(kv_own, slot, 0, me).wait_recv()
        earlier_block(slot)

    ld_copy.wait_recv()
    total_other = dot(
        jnp.sum(ld_in[...], axis=1, keepdims=True).T, head_of, EXACT
    )
    decay_other = jnp.exp(total_other)
    decay_late = jnp.exp(jnp.where(side == 0, total_other, total_own))
    decay_pair = jnp.exp(total_other + total_own)
    for k in range(chunks):
        at = slice(k * 128, (k + 1) * 128)
        s_copies[k].wait_recv()

        @pl.when(pair == 0)
        def _():
            own, other = s_own[k].astype(jnp.float32), s_in[k].astype(jnp.float32)
            early, late = jnp.where(side == 0, own, other), jnp.where(side == 0, other, own)
            p_out[k] = (decay_late[:, at] * early + late).astype(state_type)

            @pl.when(has_next)
            def _():
                p_copies[k].start()

    @pl.when(has_before)
    def _():
        to_next.wait_recv()

        @pl.when(side == 0)
        def _():
            relay_up.start()

        @pl.when(side == 1)
        def _():
            relay_down.start()

            @pl.when(has_next)
            def _():
                relay_up.start()

    @pl.when(pair >= 1)
    def _():
        own_block()

    @pl.when(pair >= 2)
    def _():
        earlier_block(1)

    @pl.when(pair >= 3)
    def _():
        arrive_and_use(0)
        arrive_and_use(2)

    @pl.when(pair >= 1)
    def _():
        for k in range(chunks):
            at = slice(k * 128, (k + 1) * 128)
            p_copies[k].wait_recv()

            @pl.when(has_next)
            def _():
                own, other = s_own[k].astype(jnp.float32), s_in[k].astype(jnp.float32)
                early, late = jnp.where(side == 0, own, other), jnp.where(side == 0, other, own)
                joined = decay_late[:, at] * early + late
                p_out[k] = (decay_pair[:, at] * p_in[k].astype(jnp.float32) + joined).astype(
                    state_type
                )
                p_copies[k].start()

    c_rows = c_ref[...]
    square = jnp.zeros((BLK, 1), jnp.float32)
    for k in range(chunks):
        at = slice(k * 128, (k + 1) * 128)
        far = dot_state(c_rows, p_in[k])
        near = dot_state(c_rows, s_in[k])
        carried = jnp.where(side == 0, far, decay_other[:, at] * far + near)
        gate = z_ref[:, at].astype(jnp.float32)
        gated = (y_ref[:, at] + carried * grow_ref[:, at]) * (gate / (1.0 + jnp.exp(-gate)))
        y_ref[:, at] = gated
        square = square + jnp.sum(gated * gated, axis=1, keepdims=True)
    inverse = lax.rsqrt(square / width + 1e-05)
    ssm_ref[...] = (y_ref[...] * inverse * gain_ref[...]).astype(jnp.bfloat16)

    @pl.when(pair == 0)
    def _():
        own_block()

    @pl.when(pair == 1)
    def _():
        earlier_block(1)

    @pl.when((pair < 3) & (me >= 1))
    def _():
        arrive_and_use(0)

    @pl.when((pair < 3) & (me >= 3))
    def _():
        arrive_and_use(2)

    for c in range(kv_heads):
        mixed = acc_ref[c] / sum_ref[c]
        for j in range(members):
            head = c * members + j
            attn_ref[:, head * HD : (head + 1) * HD] = (
                mixed[:, j * BLK : (j + 1) * BLK].T.astype(jnp.bfloat16)
            )

    ld_copy.wait_send()
    for each in s_copies:
        each.wait_send()

    @pl.when(has_next)
    def _():
        to_next.wait_send()
        for each in p_copies:
            each.wait_send()

    @pl.when(side == 0)
    def _():
        to_pair.wait_send()

    @pl.when(has_before & ((side == 0) | has_next))
    def _():
        relay_up.wait_send()

    @pl.when(has_before & (side == 1))
    def _():
        relay_down.wait_send()


def on_device(n, queries, keys, values, pattern, x_in, z_gate, bmat, cmat, log_decay, gain):
    state_type = jnp.bfloat16 if n <= 16 else jnp.float32
    heads = log_decay.shape[0]
    width = heads * P_SIZE
    chunks = width // 128
    kv_heads = keys.shape[1] // HD
    rows = queries.shape[1] // keys.shape[1] * BLK
    states = pltpu.VMEM((chunks, N, 128), state_type)
    dma = pltpu.SemaphoreType.DMA
    return pl.pallas_call(
        functools.partial(kernel, n, state_type),
        out_shape=(
            jax.ShapeDtypeStruct(queries.shape, jnp.bfloat16),
            jax.ShapeDtypeStruct(x_in.shape, jnp.bfloat16),
        ),
        in_specs=[pl.BlockSpec(memory_space=pltpu.VMEM)] * 10,
        out_specs=(pl.BlockSpec(memory_space=pltpu.VMEM),) * 2,
        scratch_shapes=[
            pltpu.VMEM((2, BLK, keys.shape[1]), jnp.bfloat16),
            pltpu.VMEM((3, 2, BLK, keys.shape[1]), jnp.bfloat16),
            pltpu.VMEM(log_decay.shape, jnp.float32),
            states, states, states, states,
            pltpu.VMEM((BLK, width), jnp.float32),
            pltpu.VMEM((BLK, width), jnp.float32),
            pltpu.VMEM((kv_heads, HD, rows), jnp.float32),
            pltpu.VMEM((kv_heads, 1, rows), jnp.float32),
            pltpu.VMEM((kv_heads, 1, rows), jnp.float32),
            dma((4,)), dma((3,)), dma, dma,
            dma((chunks,)), dma((chunks,)), dma((chunks,)), dma((chunks,)),
        ],
        compiler_params=pltpu.CompilerParams(
            collective_id=0, has_side_effects=True, vmem_limit_bytes=32 * 1024 * 1024
        ),
    )(
        queries, keys, values, pattern, x_in, z_gate, bmat, cmat, log_decay,
        gain.reshape(1, -1),
    )


def solution(mesh):
    rows = P(("groups", "ctx"), "head")
    placed = (
        rows, rows, rows, P(("groups", "ctx"), None), rows, rows, rows, rows,
        P(("groups", "head"), "ctx"), P("head"),
    )
    return jax.shard_map(
        functools.partial(on_device, mesh.shape["ctx"]),
        mesh=mesh,
        in_specs=placed,
        out_specs=(rows, rows),
        check_vma=False,
    )
```

time: 84 us -> 25 us (0.30)
  the two profiles are of different devices: /device:TPU:0 before, /device:TPU:26 now
where the time goes in v1:
time: 25 us; the launch traced here: 24.6 us
  Pallas kernels  14.6 us (58%)
  local copies, waits for them, and re-layouts  9.33 us (37%)
  between operations  0.66 us (3%)
    pallas_call x1, Pallas kernels, on_device(): pl.pallas_call(functools.partial(kernel, n, state_type), out_shape=(jax.S...  14.6 us
    unnamed x22, local copies, waits for them, and re-layouts  9.33 us

profile of v1, /device:TPU:26, one launch (start us, length us, event | category | flops | bytes accessed | tf_op | source)
XLA Modules:
  0.0 24.6 jit_solution(12401687033273314070)
XLA Ops:
  0.6 0.0 copy-start.9
  0.6 0.6 %copy-done.9 = s32[1,8]{1,0:T(1,128)S(1)} copy-done((s32[1,8]{1,0:T(1,128)S(1)}, s32[1,8]{1,0:T(1,128)}, u32[]{:S(2)}) %copy-start.9) | copy-done | bytes 56
  1.3 0.0 copy-start
  1.3 0.9 %copy-done = bf16[128,1024]{1,0:T(8,128)(2,1)S(1)} copy-done((bf16[128,1024]{1,0:T(8,128)(2,1)S(1)}, bf16[128,1024]{1,0:T(8,128)(2,1)}, u32[]{:S(2)}) %copy-start) | copy-done | bytes 262168
  2.2 0.0 copy-start.1
  2.2 0.9 %copy-done.1 = bf16[128,512]{1,0:T(8,128)(2,1)S(1)} copy-done((bf16[128,512]{1,0:T(8,128)(2,1)S(1)}, bf16[128,512]{1,0:T(8,128)(2,1)}, u32[]{:S(2)}) %copy-start.1) | copy-done | bytes 131096
  3.1 0.0 copy-start.2
  3.1 0.9 %copy-done.2 = bf16[128,512]{1,0:T(8,128)(2,1)S(1)} copy-done((bf16[128,512]{1,0:T(8,128)(2,1)S(1)}, bf16[128,512]{1,0:T(8,128)(2,1)}, u32[]{:S(2)}) %copy-start.2) | copy-done | bytes 131096
  4.0 0.0 copy-start.3
  4.1 0.8 %copy-done.3 = bf16[128,256]{1,0:T(8,128)(2,1)S(1)} copy-done((bf16[128,256]{1,0:T(8,128)(2,1)S(1)}, bf16[128,256]{1,0:T(8,128)(2,1)}, u32[]{:S(2)}) %copy-start.3) | copy-done | bytes 65560
  4.9 0.0 copy-start.4
  4.9 0.8 %copy-done.4 = bf16[128,256]{1,0:T(8,128)(2,1)S(1)} copy-done((bf16[128,256]{1,0:T(8,128)(2,1)S(1)}, bf16[128,256]{1,0:T(8,128)(2,1)}, u32[]{:S(2)}) %copy-start.4) | copy-done | bytes 65560
  5.7 0.0 copy-start.5
  5.7 0.8 %copy-done.5 = bf16[128,128]{1,0:T(8,128)(2,1)S(1)} copy-done((bf16[128,128]{1,0:T(8,128)(2,1)S(1)}, bf16[128,128]{1,0:T(8,128)(2,1)}, u32[]{:S(2)}) %copy-start.5) | copy-done | bytes 32792
  6.5 0.0 copy-start.6
  6.5 0.8 %copy-done.6 = bf16[128,128]{1,0:T(8,128)(2,1)S(1)} copy-done((bf16[128,128]{1,0:T(8,128)(2,1)S(1)}, bf16[128,128]{1,0:T(8,128)(2,1)}, u32[]{:S(2)}) %copy-start.6) | copy-done | bytes 32792
  7.2 0.0 copy-start.7
  7.2 0.7 %copy-done.7 = f32[8,128]{1,0:T(8,128)S(1)} copy-done((f32[8,128]{1,0:T(8,128)S(1)}, f32[8,128]{1,0:T(8,128)}, u32[]{:S(2)}) %copy-start.7) | copy-done | bytes 4120
  7.9 0.0 copy-start.8
  7.9 0.7 %copy-done.8 = f32[512]{0:T(512)S(1)} copy-done((f32[512]{0:T(512)S(1)}, f32[512]{0:T(512)}, u32[]{:S(2)}) %copy-start.8) | copy-done | bytes 2072
  8.6 14.6 %shard_map.113 = (bf16[128,1024]{1,0:T(8,128)(2,1)S(1)}, bf16[128,512]{1,0:T(8,128)(2,1)S(1)}) custom-call(bf16[128,1024]{1,0:T(8,128)(2,1)S(1)} %copy-done, bf16[128,256]{1,0:T(8,128)(2,1)S(1)} %copy-done.3, bf16[128,256]{1,0:T(8,128)(2,1)S(1)} %copy-done.4, s32[1,8]{1,0:T(1,128)S(1)} %copy-done.9, bf16[128,512]{1,0:T(8,128)(2,1)S(1)} %copy-done.1, ...), custom_call_target="tpu_custom_call" | custom-call | tf_op jit(solution)/shard_map/pallas_call | solution.py:311
  23.2 0.7 %copy.14 = bf16[128,1024]{1,0:T(8,128)(2,1)} copy(bf16[128,1024]{1,0:T(8,128)(2,1)S(1)} %get-tuple-element.4) | data formatting | bytes 524288
  23.9 0.7 %copy.15 = bf16[128,512]{1,0:T(8,128)(2,1)} copy(bf16[128,512]{1,0:T(8,128)(2,1)S(1)} %get-tuple-element.5) | data formatting | bytes 262144
Async XLA Ops:
  0.6 0.7 %copy-start.9 = (s32[1,8]{1,0:T(1,128)S(1)}, s32[1,8]{1,0:T(1,128)}, u32[]{:S(2)}) copy-start(s32[1,8]{1,0:T(1,128)} %pat_ref.1) | copy-start | bytes 100
  1.3 0.9 %copy-start = (bf16[128,1024]{1,0:T(8,128)(2,1)S(1)}, bf16[128,1024]{1,0:T(8,128)(2,1)}, u32[]{:S(2)}) copy-start(bf16[128,1024]{1,0:T(8,128)(2,1)} %q_ref.1) | copy-start | bytes 786436
  2.2 0.9 %copy-start.1 = (bf16[128,512]{1,0:T(8,128)(2,1)S(1)}, bf16[128,512]{1,0:T(8,128)(2,1)}, u32[]{:S(2)}) copy-start(bf16[128,512]{1,0:T(8,128)(2,1)} %x_ref.1) | copy-start | bytes 393220
  3.1 0.9 %copy-start.2 = (bf16[128,512]{1,0:T(8,128)(2,1)S(1)}, bf16[128,512]{1,0:T(8,128)(2,1)}, u32[]{:S(2)}) copy-start(bf16[128,512]{1,0:T(8,128)(2,1)} %z_ref.1) | copy-start | bytes 393220
  4.0 0.8 %copy-start.3 = (bf16[128,256]{1,0:T(8,128)(2,1)S(1)}, bf16[128,256]{1,0:T(8,128)(2,1)}, u32[]{:S(2)}) copy-start(bf16[128,256]{1,0:T(8,128)(2,1)} %k_ref.1) | copy-start | bytes 196612
  4.9 0.8 %copy-start.4 = (bf16[128,256]{1,0:T(8,128)(2,1)S(1)}, bf16[128,256]{1,0:T(8,128)(2,1)}, u32[]{:S(2)}) copy-start(bf16[128,256]{1,0:T(8,128)(2,1)} %v_ref.1) | copy-start | bytes 196612
  5.7 0.8 %copy-start.5 = (bf16[128,128]{1,0:T(8,128)(2,1)S(1)}, bf16[128,128]{1,0:T(8,128)(2,1)}, u32[]{:S(2)}) copy-start(bf16[128,128]{1,0:T(8,128)(2,1)} %b_ref.1) | copy-start | bytes 98308
  6.5 0.8 %copy-start.6 = (bf16[128,128]{1,0:T(8,128)(2,1)S(1)}, bf16[128,128]{1,0:T(8,128)(2,1)}, u32[]{:S(2)}) copy-start(bf16[128,128]{1,0:T(8,128)(2,1)} %c_ref.1) | copy-start | bytes 98308
  7.2 0.7 %copy-start.7 = (f32[8,128]{1,0:T(8,128)S(1)}, f32[8,128]{1,0:T(8,128)}, u32[]{:S(2)}) copy-start(f32[8,128]{1,0:T(8,128)} %ld_ref.1) | copy-start | bytes 12292
  7.9 0.7 %copy-start.8 = (f32[512]{0:T(512)S(1)}, f32[512]{0:T(512)}, u32[]{:S(2)}) copy-start(f32[512]{0:T(512)} %param.19) | copy-start | bytes 6148

commit v2 on v1

v2 whole, which is shorter than its diff:
```python
import functools

import jax
import jax.numpy as jnp
from jax import lax
from jax.experimental import pallas as pl
from jax.experimental.pallas import tpu as pltpu
from jax.sharding import PartitionSpec as P

BLK = 128
HD = 128
P_SIZE = 64
N = 128
UNLISTED = -1e30
EXACT = lax.Precision.HIGHEST
MESH = pl.DeviceIdType.MESH


def dot(a, b, precision=None):
    return jnp.dot(a, b, preferred_element_type=jnp.float32, precision=precision)


def dot_rows(a, b):
    return lax.dot_general(a, b, (((1,), (1,)), ((), ())), preferred_element_type=jnp.float32)


def dot_state(c, state):
    if state.dtype == jnp.bfloat16:
        return dot(c, state)
    upper = state.astype(jnp.bfloat16)
    lower = (state - upper.astype(jnp.float32)).astype(jnp.bfloat16)
    return dot(c, upper) + dot(c, lower)


def kernel(
    n, state_type,
    q_hbm, k_hbm, v_hbm, pat_hbm, x_hbm, z_hbm, b_hbm, c_hbm, ld_hbm, gain_hbm,
    acc_ref, sum_ref, ssm_ref,
    q_ref, pat_ref, x_ref, z_ref, b_ref, c_ref, ld_ref, gain_ref,
    kv_own, kv_in, ld_in, s_own, s_in, p_out, p_in, y_ref, grow_ref, max_ref,
    load_sem, kv_send, kv_recv, ld_send, ld_recv, s_send, s_recv, p_send, p_recv,
):
    me = lax.axis_index("ctx")
    pair = me // 2
    side = me % 2
    partner = me + 1 - 2 * side
    has_next = me + 2 < n
    has_before = me >= 2
    heads = ld_ref.shape[0]
    width = heads * P_SIZE
    chunks = width // 128
    kv_heads = kv_own.shape[2] // HD
    members = q_ref.shape[1] // kv_own.shape[2]

    barrier = pltpu.get_barrier_semaphore()
    for away in (-2, -1, 1, 2):
        @pl.when((me + away >= 0) & (me + away < n))
        def _():
            pl.semaphore_signal(barrier, inc=1, device_id={"ctx": me + away}, device_id_type=MESH)

    moves = (
        (ld_hbm, ld_ref), (b_hbm, b_ref), (x_hbm, x_ref), (k_hbm, kv_own.at[0]),
        (v_hbm, kv_own.at[1]), (c_hbm, c_ref), (z_hbm, z_ref), (q_hbm, q_ref),
        (gain_hbm, gain_ref), (pat_hbm, pat_ref),
    )
    loads = [pltpu.make_async_copy(src, dst, load_sem.at[i]) for i, (src, dst) in enumerate(moves)]
    for each in loads:
        each.start()
    ld_load, b_load, x_load, k_load, v_load, c_load, z_load, q_load, gain_load, pat_load = loads

    def copy(src, dst, send_sem, recv_sem, target):
        return pltpu.make_async_remote_copy(
            src_ref=src, dst_ref=dst, send_sem=send_sem, recv_sem=recv_sem,
            device_id={"ctx": target}, device_id_type=MESH,
        )

    def kv_copy(src, slot, which, target):
        return copy(src, kv_in.at[slot], kv_send.at[which], kv_recv.at[slot], target)

    to_next = kv_copy(kv_own, 1, 0, me + 2)
    to_pair = kv_copy(kv_own, 0, 1, me + 1)
    relay_up = kv_copy(kv_in.at[1], 2, 2, me + 1)
    relay_down = kv_copy(kv_in.at[1], 0, 3, me - 1)
    ld_copy = copy(ld_ref, ld_in, ld_send, ld_recv, partner)
    s_copies = [
        copy(s_own.at[k], s_in.at[k], s_send.at[k], s_recv.at[k], partner) for k in range(chunks)
    ]
    p_copies = [
        copy(p_out.at[k], p_in.at[k], p_send.at[k], p_recv.at[k], me + 2) for k in range(chunks)
    ]

    @pl.when(pair == 0)
    def _():
        p_in[...] = jnp.zeros_like(p_in)

    row = lax.broadcasted_iota(jnp.int32, (BLK, BLK), 0)
    col = lax.broadcasted_iota(jnp.int32, (BLK, BLK), 1)
    head_of = (
        lax.broadcasted_iota(jnp.int32, (heads, width), 1) // P_SIZE
        == lax.broadcasted_iota(jnp.int32, (heads, width), 0)
    ).astype(jnp.float32)

    def per_head_pair(k, matrix_of):
        x_pair = x_ref[:, k * 128 : (k + 1) * 128]
        first = dot(matrix_of(2 * k).astype(jnp.bfloat16), x_pair)
        second = dot(matrix_of(2 * k + 1).astype(jnp.bfloat16), x_pair)
        return jnp.where(col < P_SIZE, first, second)

    ld_load.wait()
    cum_row = dot(ld_ref[...], (row <= col).astype(jnp.float32), EXACT)
    total = cum_row[:, BLK - 1 :]
    fading = jnp.exp(total - cum_row)
    b_load.wait()
    b_turned = b_ref[...].astype(jnp.float32).T
    x_load.wait()
    for k in range(chunks):
        summary = per_head_pair(k, lambda h: b_turned * fading[h : h + 1, :])
        s_own[k] = summary.astype(state_type)

    peers = jnp.minimum(me, 2) + jnp.minimum(n - 1 - me, 2)
    pl.semaphore_wait(barrier, peers)

    ld_copy.start()
    for each in s_copies:
        each.start()
    k_load.wait()
    v_load.wait()

    @pl.when(has_next)
    def _():
        to_next.start()

    cum_col = cum_row.T
    c_load.wait()
    affinity = dot_rows(c_ref[...], b_ref[...])
    grow = dot(jnp.exp(cum_col), head_of, EXACT)
    z_load.wait()
    for k in range(chunks):
        at = slice(k * 128, (k + 1) * 128)

        def mixing(h):
            spread = cum_col[:, h : h + 1] - cum_row[h : h + 1, :]
            return affinity * jnp.exp(jnp.where(row >= col, spread, -jnp.inf))

        z = z_ref[:, at].astype(jnp.float32)
        gate = z / (1.0 + jnp.exp(-z))
        y_ref[:, at] = per_head_pair(k, mixing) * gate
        grow_ref[:, at] = grow[:, at] * gate
    q_load.wait()
    pat_load.wait()
    gain_load.wait()

    def head_rows(c):
        return jnp.concatenate(
            [q_ref[:, (c * members + j) * HD : (c * members + j + 1) * HD] for j in range(members)],
            axis=0,
        )

    def scores_of(keys, c):
        return dot_rows(keys, head_rows(c)) * HD ** (-0.5)

    def own_block():
        key_at = lax.broadcasted_iota(jnp.int32, (BLK, members * BLK), 0)
        query_at = lax.broadcasted_iota(jnp.int32, (BLK, members * BLK), 1) % BLK
        for c in range(kv_heads):
            scores = scores_of(kv_own[0, :, c * HD : (c + 1) * HD], c)
            scores = jnp.where(key_at <= query_at, scores, UNLISTED)
            top = jnp.max(scores, axis=0, keepdims=True)
            expo = jnp.exp(scores - top)
            v_turned = kv_own[1, :, c * HD : (c + 1) * HD].astype(jnp.float32).T.astype(jnp.bfloat16)
            acc_ref[c] = dot(v_turned, expo.astype(jnp.bfloat16))
            max_ref[c] = top
            sum_ref[c] = jnp.sum(expo, axis=0, keepdims=True)

    def earlier_block(slot):
        listed = jnp.max(
            jnp.where(pat_ref[...] == me - 1 - slot, 0.0, UNLISTED), axis=1, keepdims=True
        )
        for c in range(kv_heads):
            scores = scores_of(kv_in[slot, 0, :, c * HD : (c + 1) * HD], c) + listed
            before = max_ref[c]
            top = jnp.maximum(before, jnp.max(scores, axis=0, keepdims=True))
            scale = jnp.exp(before - top)
            expo = jnp.exp(scores - top)
            v_turned = (
                kv_in[slot, 1, :, c * HD : (c + 1) * HD].astype(jnp.float32).T.astype(jnp.bfloat16)
            )
            acc_ref[c] = acc_ref[c] * scale + dot(v_turned, expo.astype(jnp.bfloat16))
            max_ref[c] = top
            sum_ref[c] = sum_ref[c] * scale + jnp.sum(expo, axis=0, keepdims=True)

    def arrive_and_use(slot):
        if slot != 1:
            kv_copy(kv_own, slot, 0, me).wait_recv()
        earlier_block(slot)

    ld_copy.wait_recv()
    wide_own = dot(total.T, head_of, EXACT)
    wide_other = dot(jnp.sum(ld_in[...], axis=1, keepdims=True).T, head_of, EXACT)
    decay_other = jnp.exp(wide_other)
    decay_late = jnp.exp(jnp.where(side == 0, wide_other, wide_own))
    decay_pair = jnp.exp(wide_other + wide_own)

    def joined(k):
        own, other = s_own[k].astype(jnp.float32), s_in[k].astype(jnp.float32)
        early, late = jnp.where(side == 0, own, other), jnp.where(side == 0, other, own)
        return decay_late[:, k * 128 : (k + 1) * 128] * early + late

    for k in range(chunks):
        s_copies[k].wait_recv()

        @pl.when((pair == 0) & has_next)
        def _():
            p_out[k] = joined(k).astype(state_type)
            p_copies[k].start()

    @pl.when(side == 0)
    def _():
        to_pair.start()

    @pl.when(has_before)
    def _():
        to_next.wait_recv()

        @pl.when(side == 0)
        def _():
            relay_up.start()

        @pl.when(side == 1)
        def _():
            relay_down.start()

            @pl.when(has_next)
            def _():
                relay_up.start()

    @pl.when(side == 1)
    def _():
        for k in range(chunks):
            at = slice(k * 128, (k + 1) * 128)
            growth = grow_ref[:, at]
            y_ref[:, at] = y_ref[:, at] + dot_state(c_ref[...], s_in[k]) * growth
            grow_ref[:, at] = growth * decay_other[:, at]

    @pl.when(pair >= 1)
    def _():
        own_block()

    @pl.when(pair >= 2)
    def _():
        earlier_block(1)

    @pl.when(pair >= 3)
    def _():
        arrive_and_use(0)
        arrive_and_use(2)

    for k in range(chunks):
        at = slice(k * 128, (k + 1) * 128)

        @pl.when(pair >= 1)
        def _():
            p_copies[k].wait_recv()

            @pl.when(has_next)
            def _():
                p_out[k] = (
                    decay_pair[:, at] * p_in[k].astype(jnp.float32) + joined(k)
                ).astype(state_type)
                p_copies[k].start()

        y_ref[:, at] = y_ref[:, at] + dot_state(c_ref[...], p_in[k]) * grow_ref[:, at]
    gated = y_ref[...]
    square = jnp.sum(gated * gated, axis=1, keepdims=True)
    inverse = lax.rsqrt(square / width + 1e-05)
    ssm_ref[...] = (gated * inverse * gain_ref[...]).astype(jnp.bfloat16)

    @pl.when(pair == 0)
    def _():
        own_block()

    @pl.when(pair == 1)
    def _():
        earlier_block(1)

    @pl.when((pair < 3) & (me >= 1))
    def _():
        arrive_and_use(0)

    @pl.when((pair < 3) & (me >= 3))
    def _():
        arrive_and_use(2)

    ld_copy.wait_send()
    for each in s_copies:
        each.wait_send()

    @pl.when(has_next)
    def _():
        to_next.wait_send()
        for each in p_copies:
            each.wait_send()

    @pl.when(side == 0)
    def _():
        to_pair.wait_send()

    @pl.when(has_before & ((side == 0) | has_next))
    def _():
        relay_up.wait_send()

    @pl.when(has_before & (side == 1))
    def _():
        relay_down.wait_send()


def finish(acc_ref, sum_ref, ssm_ref, attn_hbm, ssm_hbm, attn_ref, sems):
    kv_heads, _, rows = acc_ref.shape
    ssm_copy = pltpu.make_async_copy(ssm_ref, ssm_hbm, sems.at[kv_heads])
    ssm_copy.start()
    copies = []
    for c in range(kv_heads):
        mixed = acc_ref[c] / sum_ref[c]
        for j in range(rows // BLK):
            head = c * (rows // BLK) + j
            attn_ref[:, head * HD : (head + 1) * HD] = (
                mixed[:, j * BLK : (j + 1) * BLK].T.astype(jnp.bfloat16)
            )
        at = pl.ds(c * rows, rows)
        copies.append(
            pltpu.make_async_copy(attn_ref.at[:, at], attn_hbm.at[:, at], sems.at[c])
        )
        copies[-1].start()
    for each in copies:
        each.wait()
    ssm_copy.wait()


def on_device(n, queries, keys, values, pattern, x_in, z_gate, bmat, cmat, log_decay, gain):
    state_type = jnp.bfloat16 if n <= 16 else jnp.float32
    heads = log_decay.shape[0]
    width = heads * P_SIZE
    chunks = width // 128
    kv_heads = keys.shape[1] // HD
    rows = queries.shape[1] // keys.shape[1] * BLK
    states = pltpu.VMEM((chunks, N, 128), state_type)
    dma = pltpu.SemaphoreType.DMA
    in_hbm = pl.BlockSpec(memory_space=pltpu.HBM)
    in_vmem = pl.BlockSpec(memory_space=pltpu.VMEM)

    def held(array):
        return pltpu.VMEM(array.shape, array.dtype)

    gain = gain.reshape(1, -1)
    far_inputs = [
        pltpu.with_memory_space_constraint(each, pltpu.HBM)
        for each in (queries, keys, values, pattern, x_in, z_gate, bmat, cmat, log_decay, gain)
    ]
    unscaled, totals, ssm = pl.pallas_call(
        functools.partial(kernel, n, state_type),
        out_shape=(
            jax.ShapeDtypeStruct((kv_heads, HD, rows), jnp.float32),
            jax.ShapeDtypeStruct((kv_heads, 1, rows), jnp.float32),
            jax.ShapeDtypeStruct(x_in.shape, jnp.bfloat16),
        ),
        in_specs=[in_hbm] * 10,
        out_specs=(in_vmem,) * 3,
        scratch_shapes=[
            held(queries), held(pattern), held(x_in), held(z_gate), held(bmat), held(cmat),
            held(log_decay), held(gain),
            pltpu.VMEM((2, BLK, keys.shape[1]), jnp.bfloat16),
            pltpu.VMEM((3, 2, BLK, keys.shape[1]), jnp.bfloat16),
            pltpu.VMEM(log_decay.shape, jnp.float32),
            states, states, states, states,
            pltpu.VMEM((BLK, width), jnp.float32),
            pltpu.VMEM((BLK, width), jnp.float32),
            pltpu.VMEM((kv_heads, 1, rows), jnp.float32),
            dma((10,)), dma((4,)), dma((3,)), dma, dma,
            dma((chunks,)), dma((chunks,)), dma((chunks,)), dma((chunks,)),
        ],
        compiler_params=pltpu.CompilerParams(
            collective_id=0, has_side_effects=True, vmem_limit_bytes=32 * 1024 * 1024
        ),
    )(*far_inputs)
    return pl.pallas_call(
        finish,
        out_shape=(
            jax.ShapeDtypeStruct(queries.shape, jnp.bfloat16),
            jax.ShapeDtypeStruct(x_in.shape, jnp.bfloat16),
        ),
        in_specs=[in_vmem] * 3,
        out_specs=(in_hbm, in_hbm),
        scratch_shapes=[held(queries), dma((kv_heads + 1,))],
        compiler_params=pltpu.CompilerParams(vmem_limit_bytes=32 * 1024 * 1024),
    )(unscaled, totals, ssm)


def solution(mesh):
    rows = P(("groups", "ctx"), "head")
    placed = (
        rows, rows, rows, P(("groups", "ctx"), None), rows, rows, rows, rows,
        P(("groups", "head"), "ctx"), P("head"),
    )
    return jax.shard_map(
        functools.partial(on_device, mesh.shape["ctx"]),
        mesh=mesh,
        in_specs=placed,
        out_specs=(rows, rows),
        check_vma=False,
    )
```

time: 25 us -> 16.6 us (0.66)
  the two profiles are of different devices: /device:TPU:26 before, /device:TPU:24 now
where the time goes in v2:
time: 16.6 us; the launch traced here: 16.3 us
  Pallas kernels  15.7 us (95%)
  between operations  0.64 us (4%)
    pallas_call x1, Pallas kernels, on_device(): pl.pallas_call(functools.partial(kernel, n, state_type), out_shape=(jax.S...  14.8 us
    pallas_call x1, Pallas kernels, on_device(): pl.pallas_call(finish, out_shape=(jax.ShapeDtypeStruct(queries.shape, jnp...  0.84 us

profile of v2, /device:TPU:24, one launch (start us, length us, event | category | flops | bytes accessed | tf_op | source)
XLA Modules:
  0.0 16.3 jit_solution(12873756341866340629)
XLA Ops:
  0.6 14.8 %shard_map.113 = (f32[2,128,512]{2,1,0:T(8,128)S(1)}, f32[2,1,512]{2,1,0:T(1,128)S(1)}, bf16[128,512]{1,0:T(8,128)(2,1)S(1)}) custom-call(bf16[128,1024]{1,0:T(8,128)(2,1)} %q_hbm.1, bf16[128,256]{1,0:T(8,128)(2,1)} %k_hbm.1, bf16[128,256]{1,0:T(8,128)(2,1)} %v_hbm.1, s32[1,8]{1,0:T(1,128)} %pat_hbm.1, bf16[128,512]{1,0:T(8,128)(2,1)} %x_hbm.1, ...), custom_call_target="tpu_custom_call" | custom-call | tf_op jit(solution)/shard_map/pallas_call | solution.py:359
  15.5 0.8 %shard_map.114 = (bf16[128,1024]{1,0:T(8,128)(2,1)}, bf16[128,512]{1,0:T(8,128)(2,1)}) custom-call(f32[2,128,512]{2,1,0:T(8,128)S(1)} %get-tuple-element.5.acc_ref, f32[2,1,512]{2,1,0:T(1,128)S(1)} %get-tuple-element.6.sum_ref, bf16[128,512]{1,0:T(8,128)(2,1)S(1)} %get-tuple-element.7.ssm_ref), custom_call_target="tpu_custom_call" | custom-call | tf_op jit(solution)/shard_map/pallas_call | solution.py:385

commit v3 on v2

--- a/solution.py
+++ b/solution.py
@@ -37,7 +37,7 @@
     q_hbm, k_hbm, v_hbm, pat_hbm, x_hbm, z_hbm, b_hbm, c_hbm, ld_hbm, gain_hbm,
     acc_ref, sum_ref, ssm_ref,
     q_ref, pat_ref, x_ref, z_ref, b_ref, c_ref, ld_ref, gain_ref,
-    kv_own, kv_in, ld_in, s_own, s_in, p_out, p_in, y_ref, grow_ref, max_ref,
+    kv_own, kv_in, ld_in, s_own, s_in, p_out, p_in, joint_ref, y_ref, grow_ref, max_ref,
     load_sem, kv_send, kv_recv, ld_send, ld_recv, s_send, s_recv, p_send, p_recv,
 ):
     me = lax.axis_index("ctx")
@@ -53,20 +53,21 @@
     members = q_ref.shape[1] // kv_own.shape[2]
 
     barrier = pltpu.get_barrier_semaphore()
-    for away in (-2, -1, 1, 2):
+    pl.semaphore_signal(barrier, inc=1, device_id={"ctx": partner}, device_id_type=MESH)
+    for away in (-2, 2):
         @pl.when((me + away >= 0) & (me + away < n))
         def _():
             pl.semaphore_signal(barrier, inc=1, device_id={"ctx": me + away}, device_id_type=MESH)
 
     moves = (
-        (ld_hbm, ld_ref), (b_hbm, b_ref), (x_hbm, x_ref), (k_hbm, kv_own.at[0]),
-        (v_hbm, kv_own.at[1]), (c_hbm, c_ref), (z_hbm, z_ref), (q_hbm, q_ref),
+        (k_hbm, kv_own.at[0]), (v_hbm, kv_own.at[1]), (ld_hbm, ld_ref), (b_hbm, b_ref),
+        (x_hbm, x_ref), (c_hbm, c_ref), (z_hbm, z_ref), (q_hbm, q_ref),
         (gain_hbm, gain_ref), (pat_hbm, pat_ref),
     )
     loads = [pltpu.make_async_copy(src, dst, load_sem.at[i]) for i, (src, dst) in enumerate(moves)]
     for each in loads:
         each.start()
-    ld_load, b_load, x_load, k_load, v_load, c_load, z_load, q_load, gain_load, pat_load = loads
+    k_load, v_load, ld_load, b_load, x_load, c_load, z_load, q_load, gain_load, pat_load = loads
 
     def copy(src, dst, send_sem, recv_sem, target):
         return pltpu.make_async_remote_copy(
@@ -74,13 +75,20 @@
             device_id={"ctx": target}, device_id_type=MESH,
         )
 
-    def kv_copy(src, slot, which, target):
-        return copy(src, kv_in.at[slot], kv_send.at[which], kv_recv.at[slot], target)
-
-    to_next = kv_copy(kv_own, 1, 0, me + 2)
-    to_pair = kv_copy(kv_own, 0, 1, me + 1)
-    relay_up = kv_copy(kv_in.at[1], 2, 2, me + 1)
-    relay_down = kv_copy(kv_in.at[1], 0, 3, me - 1)
+    def kv_copies(src, slot, which, target):
+        return [
+            copy(
+                src.at[half], kv_in.at[slot, half], kv_send.at[which, half],
+                kv_recv.at[slot, half], target,
+            )
+            for half in (0, 1)
+        ]
+
+    to_next = kv_copies(kv_own, 1, 0, me + 2)
+    to_pair = kv_copies(kv_own, 0, 1, partner)
+    relay_down = kv_copies(kv_in.at[1], 0, 2, partner)
+    forward = kv_copies(kv_in.at[0], 2, 3, me + 2)
+    forwards = has_next & (me >= 1)
     ld_copy = copy(ld_ref, ld_in, ld_send, ld_recv, partner)
     s_copies = [
         copy(s_own.at[k], s_in.at[k], s_send.at[k], s_recv.at[k], partner) for k in range(chunks)
@@ -112,23 +120,28 @@
     fading = jnp.exp(total - cum_row)
     b_load.wait()
     b_turned = b_ref[...].astype(jnp.float32).T
+
+    peers = 1 + has_before.astype(jnp.int32) + has_next.astype(jnp.int32)
+    pl.semaphore_wait(barrier, peers)
+    k_load.wait()
+    v_load.wait()
+
+    @pl.when(has_next)
+    def _():
+        for each in to_next:
+            each.start()
+
+    ld_copy.start()
     x_load.wait()
     for k in range(chunks):
         summary = per_head_pair(k, lambda h: b_turned * fading[h : h + 1, :])
         s_own[k] = summary.astype(state_type)
-
-    peers = jnp.minimum(me, 2) + jnp.minimum(n - 1 - me, 2)
-    pl.semaphore_wait(barrier, peers)
-
-    ld_copy.start()
-    for each in s_copies:
-        each.start()
-    k_load.wait()
-    v_load.wait()
-
-    @pl.when(has_next)
-    def _():
-        to_next.start()
+        s_copies[k].start()
+
+    @pl.when(side == 0)
+    def _():
+        for each in to_pair:
+            each.start()
 
     cum_col = cum_row.T
     c_load.wait()
@@ -189,11 +202,6 @@
             max_ref[c] = top
             sum_ref[c] = sum_ref[c] * scale + jnp.sum(expo, axis=0, keepdims=True)
 
-    def arrive_and_use(slot):
-        if slot != 1:
-            kv_copy(kv_own, slot, 0, me).wait_recv()
-        earlier_block(slot)
-
     ld_copy.wait_recv()
     wide_own = dot(total.T, head_of, EXACT)
     wide_other = dot(jnp.sum(ld_in[...], axis=1, keepdims=True).T, head_of, EXACT)
@@ -208,31 +216,25 @@
 
     for k in range(chunks):
         s_copies[k].wait_recv()
+        joint = joined(k)
 
         @pl.when((pair == 0) & has_next)
         def _():
-            p_out[k] = joined(k).astype(state_type)
+            p_out[k] = joint.astype(state_type)
             p_copies[k].start()
 
-    @pl.when(side == 0)
-    def _():
-        to_pair.start()
+        @pl.when((pair >= 1) & has_next)
+        def _():
+            joint_ref[k] = joint
 
     @pl.when(has_before)
     def _():
-        to_next.wait_recv()
-
-        @pl.when(side == 0)
-        def _():
-            relay_up.start()
-
-        @pl.when(side == 1)
-        def _():
-            relay_down.start()
-
-            @pl.when(has_next)
+        for half in (0, 1):
+            to_next[half].wait_recv()
+
+            @pl.when(side == 1)
             def _():
-                relay_up.start()
+                relay_down[half].start()
 
     @pl.when(side == 1)
     def _():
@@ -242,18 +244,23 @@
             y_ref[:, at] = y_ref[:, at] + dot_state(c_ref[...], s_in[k]) * growth
             grow_ref[:, at] = growth * decay_other[:, at]
 
-    @pl.when(pair >= 1)
+    def pass_on(half):
+        to_pair[half].wait_recv()
+
+        @pl.when(forwards)
+        def _():
+            forward[half].start()
+
+    @pl.when(pair >= 2)
     def _():
         own_block()
-
-    @pl.when(pair >= 2)
-    def _():
         earlier_block(1)
+        pass_on(0)
 
     @pl.when(pair >= 3)
     def _():
-        arrive_and_use(0)
-        arrive_and_use(2)
+        pass_on(1)
+        earlier_block(0)
 
     for k in range(chunks):
         at = slice(k * 128, (k + 1) * 128)
@@ -265,31 +272,44 @@
             @pl.when(has_next)
             def _():
                 p_out[k] = (
-                    decay_pair[:, at] * p_in[k].astype(jnp.float32) + joined(k)
+                    decay_pair[:, at] * p_in[k].astype(jnp.float32) + joint_ref[k]
                 ).astype(state_type)
                 p_copies[k].start()
 
+        if k == min(1, chunks - 1):
+            @pl.when(pair == 2)
+            def _():
+                pass_on(1)
+
         y_ref[:, at] = y_ref[:, at] + dot_state(c_ref[...], p_in[k]) * grow_ref[:, at]
+
+    @pl.when(pair < 2)
+    def _():
+        own_block()
+
+        @pl.when(me >= 1)
+        def _():
+            pass_on(0)
+            pass_on(1)
+
     gated = y_ref[...]
     square = jnp.sum(gated * gated, axis=1, keepdims=True)
     inverse = lax.rsqrt(square / width + 1e-05)
     ssm_ref[...] = (gated * inverse * gain_ref[...]).astype(jnp.bfloat16)
 
-    @pl.when(pair == 0)
-    def _():
-        own_block()
-
     @pl.when(pair == 1)
     def _():
         earlier_block(1)
 
     @pl.when((pair < 3) & (me >= 1))
     def _():
-        arrive_and_use(0)
-
-    @pl.when((pair < 3) & (me >= 3))
-    def _():
-        arrive_and_use(2)
+        earlier_block(0)
+
+    @pl.when(me >= 3)
+    def _():
+        for each in forward:
+            each.wait_recv()
+        earlier_block(2)
 
     ld_copy.wait_send()
     for each in s_copies:
@@ -297,21 +317,23 @@
 
     @pl.when(has_next)
     def _():
-        to_next.wait_send()
-        for each in p_copies:
+        for each in to_next + p_copies:
             each.wait_send()
 
     @pl.when(side == 0)
     def _():
-        to_pair.wait_send()
-
-    @pl.when(has_before & ((side == 0) | has_next))
-    def _():
-        relay_up.wait_send()
+        for each in to_pair:
+            each.wait_send()
 
     @pl.when(has_before & (side == 1))
     def _():
-        relay_down.wait_send()
+        for each in relay_down:
+            each.wait_send()
+
+    @pl.when(forwards)
+    def _():
+        for each in forward:
+            each.wait_send()
 
 
 def finish(acc_ref, sum_ref, ssm_ref, attn_hbm, ssm_hbm, attn_ref, sems):
@@ -372,10 +394,11 @@
             pltpu.VMEM((3, 2, BLK, keys.shape[1]), jnp.bfloat16),
             pltpu.VMEM(log_decay.shape, jnp.float32),
             states, states, states, states,
+            pltpu.VMEM((chunks, N, 128), jnp.float32),
             pltpu.VMEM((BLK, width), jnp.float32),
             pltpu.VMEM((BLK, width), jnp.float32),
             pltpu.VMEM((kv_heads, 1, rows), jnp.float32),
-            dma((10,)), dma((4,)), dma((3,)), dma, dma,
+            dma((10,)), dma((4, 2)), dma((3, 2)), dma, dma,
             dma((chunks,)), dma((chunks,)), dma((chunks,)), dma((chunks,)),
         ],
         compiler_params=pltpu.CompilerParams(

time: 16.6 us -> 18.2 us (1.096)
  Pallas kernels: 15.7 us -> 17.4 us
    pallas_call x1, Pallas kernels: 14.8 us -> 16.6 us  [on_device(): pl.pallas_call(functools.partial(kernel, n, state_type), out_shape=(jax.S...]
where the time goes in v3:
time: 18.2 us; the launch traced here: 18.1 us
  Pallas kernels  17.4 us (96%)
  between operations  0.64 us (4%)
    pallas_call x1, Pallas kernels, on_device(): pl.pallas_call(functools.partial(kernel, n, state_type), out_shape=(jax.S...  16.6 us
    pallas_call x1, Pallas kernels, on_device(): pl.pallas_call(finish, out_shape=(jax.ShapeDtypeStruct(queries.shape, jnp...  0.84 us

profile of v3, /device:TPU:24, one launch (start us, length us, event | category | flops | bytes accessed | tf_op | source)
XLA Modules:
  0.0 18.1 jit_solution(12245455861766118882)
XLA Ops:
  0.6 16.6 %shard_map.113 = (f32[2,128,512]{2,1,0:T(8,128)S(1)}, f32[2,1,512]{2,1,0:T(1,128)S(1)}, bf16[128,512]{1,0:T(8,128)(2,1)S(1)}) custom-call(bf16[128,1024]{1,0:T(8,128)(2,1)} %q_hbm.1, bf16[128,256]{1,0:T(8,128)(2,1)} %k_hbm.1, bf16[128,256]{1,0:T(8,128)(2,1)} %v_hbm.1, s32[1,8]{1,0:T(1,128)} %pat_hbm.1, bf16[128,512]{1,0:T(8,128)(2,1)} %x_hbm.1, ...), custom_call_target="tpu_custom_call" | custom-call | tf_op jit(solution)/shard_map/pallas_call | solution.py:381
  17.2 0.8 %shard_map.114 = (bf16[128,1024]{1,0:T(8,128)(2,1)}, bf16[128,512]{1,0:T(8,128)(2,1)}) custom-call(f32[2,128,512]{2,1,0:T(8,128)S(1)} %get-tuple-element.5.acc_ref, f32[2,1,512]{2,1,0:T(1,128)S(1)} %get-tuple-element.6.sum_ref, bf16[128,512]{1,0:T(8,128)(2,1)S(1)} %get-tuple-element.7.ssm_ref), custom_call_target="tpu_custom_call" | custom-call | tf_op jit(solution)/shard_map/pallas_call | solution.py:408

commit v4 on v3

--- a/solution.py
+++ b/solution.py
@@ -123,14 +123,6 @@
 
     peers = 1 + has_before.astype(jnp.int32) + has_next.astype(jnp.int32)
     pl.semaphore_wait(barrier, peers)
-    k_load.wait()
-    v_load.wait()
-
-    @pl.when(has_next)
-    def _():
-        for each in to_next:
-            each.start()
-
     ld_copy.start()
     x_load.wait()
     for k in range(chunks):
@@ -138,9 +130,12 @@
         s_own[k] = summary.astype(state_type)
         s_copies[k].start()
 
-    @pl.when(side == 0)
-    def _():
-        for each in to_pair:
+    k_load.wait()
+    v_load.wait()
+
+    @pl.when(has_next)
+    def _():
+        for each in to_next:
             each.start()
 
     cum_col = cum_row.T
@@ -227,6 +222,11 @@
         def _():
             joint_ref[k] = joint
 
+    @pl.when(side == 0)
+    def _():
+        for each in to_pair:
+            each.start()
+
     @pl.when(has_before)
     def _():
         for half in (0, 1):
@@ -255,10 +255,10 @@
     def _():
         own_block()
         earlier_block(1)
+
+    @pl.when(pair >= 3)
+    def _():
         pass_on(0)
-
-    @pl.when(pair >= 3)
-    def _():
         pass_on(1)
         earlier_block(0)
 
@@ -276,21 +276,16 @@
                 ).astype(state_type)
                 p_copies[k].start()
 
-        if k == min(1, chunks - 1):
-            @pl.when(pair == 2)
-            def _():
-                pass_on(1)
-
         y_ref[:, at] = y_ref[:, at] + dot_state(c_ref[...], p_in[k]) * grow_ref[:, at]
 
     @pl.when(pair < 2)
     def _():
         own_block()
 
-        @pl.when(me >= 1)
-        def _():
-            pass_on(0)
-            pass_on(1)
+    @pl.when((pair < 3) & (me >= 1))
+    def _():
+        pass_on(0)
+        pass_on(1)
 
     gated = y_ref[...]
     square = jnp.sum(gated * gated, axis=1, keepdims=True)

time: 18.2 us -> 18.8 us (1.033)
  the two profiles are of different devices: /device:TPU:24 before, /device:TPU:26 now
where the time goes in v4:
time: 18.8 us; the launch traced here: 18.6 us
  Pallas kernels  18 us (96%)
  between operations  0.64 us (3%)
    pallas_call x1, Pallas kernels, on_device(): pl.pallas_call(functools.partial(kernel, n, state_type), out_shape=(jax.S...  17.2 us
    pallas_call x1, Pallas kernels, on_device(): pl.pallas_call(finish, out_shape=(jax.ShapeDtypeStruct(queries.shape, jnp...  0.84 us

profile of v4, /device:TPU:26, one launch (start us, length us, event | category | flops | bytes accessed | tf_op | source)
XLA Modules:
  0.0 18.6 jit_solution(13933201997441183476)
XLA Ops:
  0.6 17.2 %shard_map.113 = (f32[2,128,512]{2,1,0:T(8,128)S(1)}, f32[2,1,512]{2,1,0:T(1,128)S(1)}, bf16[128,512]{1,0:T(8,128)(2,1)S(1)}) custom-call(bf16[128,1024]{1,0:T(8,128)(2,1)} %q_hbm.1, bf16[128,256]{1,0:T(8,128)(2,1)} %k_hbm.1, bf16[128,256]{1,0:T(8,128)(2,1)} %v_hbm.1, s32[1,8]{1,0:T(1,128)} %pat_hbm.1, bf16[128,512]{1,0:T(8,128)(2,1)} %x_hbm.1, ...), custom_call_target="tpu_custom_call" | custom-call | tf_op jit(solution)/shard_map/pallas_call | solution.py:376
  17.8 0.8 %shard_map.114 = (bf16[128,1024]{1,0:T(8,128)(2,1)}, bf16[128,512]{1,0:T(8,128)(2,1)}) custom-call(f32[2,128,512]{2,1,0:T(8,128)S(1)} %get-tuple-element.5.acc_ref, f32[2,1,512]{2,1,0:T(1,128)S(1)} %get-tuple-element.6.sum_ref, bf16[128,512]{1,0:T(8,128)(2,1)S(1)} %get-tuple-element.7.ssm_ref), custom_call_target="tpu_custom_call" | custom-call | tf_op jit(solution)/shard_map/pallas_call | solution.py:403

commit v5 on v3

--- a/solution.py
+++ b/solution.py
@@ -120,27 +120,22 @@
     fading = jnp.exp(total - cum_row)
     b_load.wait()
     b_turned = b_ref[...].astype(jnp.float32).T
-
-    peers = 1 + has_before.astype(jnp.int32) + has_next.astype(jnp.int32)
-    pl.semaphore_wait(barrier, peers)
-    k_load.wait()
-    v_load.wait()
-
-    @pl.when(has_next)
-    def _():
-        for each in to_next:
-            each.start()
-
-    ld_copy.start()
     x_load.wait()
     for k in range(chunks):
         summary = per_head_pair(k, lambda h: b_turned * fading[h : h + 1, :])
         s_own[k] = summary.astype(state_type)
-        s_copies[k].start()
-
-    @pl.when(side == 0)
-    def _():
-        for each in to_pair:
+
+    peers = 1 + has_before.astype(jnp.int32) + has_next.astype(jnp.int32)
+    pl.semaphore_wait(barrier, peers)
+    ld_copy.start()
+    for each in s_copies:
+        each.start()
+    k_load.wait()
+    v_load.wait()
+
+    @pl.when(has_next)
+    def _():
+        for each in to_next:
             each.start()
 
     cum_col = cum_row.T
@@ -226,6 +221,11 @@
         @pl.when((pair >= 1) & has_next)
         def _():
             joint_ref[k] = joint
+
+    @pl.when(side == 0)
+    def _():
+        for each in to_pair:
+            each.start()
 
     @pl.when(has_before)
     def _():

time: 18.2 us -> 17.9 us (0.984)
  Pallas kernels: 17.4 us -> 17.1 us
    pallas_call x1, Pallas kernels: 16.6 us -> 16.2 us  [on_device(): pl.pallas_call(functools.partial(kernel, n, state_type), out_shape=(jax.S...]
where the time goes in v5:
time: 17.9 us; the launch traced here: 17.7 us
  Pallas kernels  17.1 us (96%)
  between operations  0.64 us (4%)
    pallas_call x1, Pallas kernels, on_device(): pl.pallas_call(functools.partial(kernel, n, state_type), out_shape=(jax.S...  16.2 us
    pallas_call x1, Pallas kernels, on_device(): pl.pallas_call(finish, out_shape=(jax.ShapeDtypeStruct(queries.shape, jnp...  0.84 us

profile of v5, /device:TPU:24, one launch (start us, length us, event | category | flops | bytes accessed | tf_op | source)
XLA Modules:
  0.0 17.7 jit_solution(15437487063992704889)
XLA Ops:
  0.6 16.2 %shard_map.113 = (f32[2,128,512]{2,1,0:T(8,128)S(1)}, f32[2,1,512]{2,1,0:T(1,128)S(1)}, bf16[128,512]{1,0:T(8,128)(2,1)S(1)}) custom-call(bf16[128,1024]{1,0:T(8,128)(2,1)} %q_hbm.1, bf16[128,256]{1,0:T(8,128)(2,1)} %k_hbm.1, bf16[128,256]{1,0:T(8,128)(2,1)} %v_hbm.1, s32[1,8]{1,0:T(1,128)} %pat_hbm.1, bf16[128,512]{1,0:T(8,128)(2,1)} %x_hbm.1, ...), custom_call_target="tpu_custom_call" | custom-call | tf_op jit(solution)/shard_map/pallas_call | solution.py:381
  16.9 0.8 %shard_map.114 = (bf16[128,1024]{1,0:T(8,128)(2,1)}, bf16[128,512]{1,0:T(8,128)(2,1)}) custom-call(f32[2,128,512]{2,1,0:T(8,128)S(1)} %get-tuple-element.5.acc_ref, f32[2,1,512]{2,1,0:T(1,128)S(1)} %get-tuple-element.6.sum_ref, bf16[128,512]{1,0:T(8,128)(2,1)S(1)} %get-tuple-element.7.ssm_ref), custom_call_target="tpu_custom_call" | custom-call | tf_op jit(solution)/shard_map/pallas_call | solution.py:408

commit v6 on v2

--- a/solution.py
+++ b/solution.py
@@ -74,13 +74,19 @@
             device_id={"ctx": target}, device_id_type=MESH,
         )
 
-    def kv_copy(src, slot, which, target):
-        return copy(src, kv_in.at[slot], kv_send.at[which], kv_recv.at[slot], target)
-
-    to_next = kv_copy(kv_own, 1, 0, me + 2)
-    to_pair = kv_copy(kv_own, 0, 1, me + 1)
-    relay_up = kv_copy(kv_in.at[1], 2, 2, me + 1)
-    relay_down = kv_copy(kv_in.at[1], 0, 3, me - 1)
+    def kv_copies(src, slot, which, target):
+        return [
+            copy(
+                src.at[half], kv_in.at[slot, half], kv_send.at[which, half],
+                kv_recv.at[slot, half], target,
+            )
+            for half in (0, 1)
+        ]
+
+    to_next = kv_copies(kv_own, 1, 0, me + 2)
+    to_pair = kv_copies(kv_own, 0, 1, me + 1)
+    relay_up = kv_copies(kv_in.at[1], 2, 2, me + 1)
+    relay_down = kv_copies(kv_in.at[1], 0, 3, me - 1)
     ld_copy = copy(ld_ref, ld_in, ld_send, ld_recv, partner)
     s_copies = [
         copy(s_own.at[k], s_in.at[k], s_send.at[k], s_recv.at[k], partner) for k in range(chunks)
@@ -128,7 +134,8 @@
 
     @pl.when(has_next)
     def _():
-        to_next.start()
+        for each in to_next:
+            each.start()
 
     cum_col = cum_row.T
     c_load.wait()
@@ -191,7 +198,8 @@
 
     def arrive_and_use(slot):
         if slot != 1:
-            kv_copy(kv_own, slot, 0, me).wait_recv()
+            for each in kv_copies(kv_own, slot, 0, me):
+                each.wait_recv()
         earlier_block(slot)
 
     ld_copy.wait_recv()
@@ -216,23 +224,21 @@
 
     @pl.when(side == 0)
     def _():
-        to_pair.start()
+        for each in to_pair:
+            each.start()
 
     @pl.when(has_before)
     def _():
-        to_next.wait_recv()
-
-        @pl.when(side == 0)
-        def _():
-            relay_up.start()
-
-        @pl.when(side == 1)
-        def _():
-            relay_down.start()
-
-            @pl.when(has_next)
+        for half in (0, 1):
+            to_next[half].wait_recv()
+
+            @pl.when((side == 0) | has_next)
             def _():
-                relay_up.start()
+                relay_up[half].start()
+
+            @pl.when(side == 1)
+            def _():
+                relay_down[half].start()
 
     @pl.when(side == 1)
     def _():
@@ -242,7 +248,7 @@
             y_ref[:, at] = y_ref[:, at] + dot_state(c_ref[...], s_in[k]) * growth
             grow_ref[:, at] = growth * decay_other[:, at]
 
-    @pl.when(pair >= 1)
+    @pl.when(pair >= 2)
     def _():
         own_block()
 
@@ -275,7 +281,7 @@
     inverse = lax.rsqrt(square / width + 1e-05)
     ssm_ref[...] = (gated * inverse * gain_ref[...]).astype(jnp.bfloat16)
 
-    @pl.when(pair == 0)
+    @pl.when(pair < 2)
     def _():
         own_block()
 
@@ -297,21 +303,23 @@
 
     @pl.when(has_next)
     def _():
-        to_next.wait_send()
-        for each in p_copies:
+        for each in to_next + p_copies:
             each.wait_send()
 
     @pl.when(side == 0)
     def _():
-        to_pair.wait_send()
+        for each in to_pair:
+            each.wait_send()
 
     @pl.when(has_before & ((side == 0) | has_next))
     def _():
-        relay_up.wait_send()
+        for each in relay_up:
+            each.wait_send()
 
     @pl.when(has_before & (side == 1))
     def _():
-        relay_down.wait_send()
+        for each in relay_down:
+            each.wait_send()
 
 
 def finish(acc_ref, sum_ref, ssm_ref, attn_hbm, ssm_hbm, attn_ref, sems):
@@ -375,7 +383,7 @@
             pltpu.VMEM((BLK, width), jnp.float32),
             pltpu.VMEM((BLK, width), jnp.float32),
             pltpu.VMEM((kv_heads, 1, rows), jnp.float32),
-            dma((10,)), dma((4,)), dma((3,)), dma, dma,
+            dma((10,)), dma((4, 2)), dma((3, 2)), dma, dma,
             dma((chunks,)), dma((chunks,)), dma((chunks,)), dma((chunks,)),
         ],
         compiler_params=pltpu.CompilerParams(

time: 16.6 us -> 16.6 us (level)
  no operation moved by 1% of the time
where the time goes in v6:
time: 16.6 us; the launch traced here: 16.4 us
  Pallas kernels  15.8 us (95%)
  between operations  0.64 us (4%)
    pallas_call x1, Pallas kernels, on_device(): pl.pallas_call(functools.partial(kernel, n, state_type), out_shape=(jax.S...  14.9 us
    pallas_call x1, Pallas kernels, on_device(): pl.pallas_call(finish, out_shape=(jax.ShapeDtypeStruct(queries.shape, jnp...  0.84 us

profile of v6, /device:TPU:24, one launch (start us, length us, event | category | flops | bytes accessed | tf_op | source)
XLA Modules:
  0.0 16.4 jit_solution(15889707193636993235)
XLA Ops:
  0.6 14.9 %shard_map.113 = (f32[2,128,512]{2,1,0:T(8,128)S(1)}, f32[2,1,512]{2,1,0:T(1,128)S(1)}, bf16[128,512]{1,0:T(8,128)(2,1)S(1)}) custom-call(bf16[128,1024]{1,0:T(8,128)(2,1)} %q_hbm.1, bf16[128,256]{1,0:T(8,128)(2,1)} %k_hbm.1, bf16[128,256]{1,0:T(8,128)(2,1)} %v_hbm.1, s32[1,8]{1,0:T(1,128)} %pat_hbm.1, bf16[128,512]{1,0:T(8,128)(2,1)} %x_hbm.1, ...), custom_call_target="tpu_custom_call" | custom-call | tf_op jit(solution)/shard_map/pallas_call | solution.py:367
  15.6 0.8 %shard_map.114 = (bf16[128,1024]{1,0:T(8,128)(2,1)}, bf16[128,512]{1,0:T(8,128)(2,1)}) custom-call(f32[2,128,512]{2,1,0:T(8,128)S(1)} %get-tuple-element.5.acc_ref, f32[2,1,512]{2,1,0:T(1,128)S(1)} %get-tuple-element.6.sum_ref, bf16[128,512]{1,0:T(8,128)(2,1)S(1)} %get-tuple-element.7.ssm_ref), custom_call_target="tpu_custom_call" | custom-call | tf_op jit(solution)/shard_map/pallas_call | solution.py:393

commit v7 on v6

--- a/solution.py
+++ b/solution.py
@@ -259,7 +259,6 @@
     @pl.when(pair >= 3)
     def _():
         arrive_and_use(0)
-        arrive_and_use(2)
 
     for k in range(chunks):
         at = slice(k * 128, (k + 1) * 128)
@@ -293,7 +292,7 @@
     def _():
         arrive_and_use(0)
 
-    @pl.when((pair < 3) & (me >= 3))
+    @pl.when(me >= 3)
     def _():
         arrive_and_use(2)
 

time: 16.6 us -> 16.9 us (1.018)
  the two profiles are of different devices: /device:TPU:24 before, /device:TPU:26 now
where the time goes in v7:
time: 16.9 us; the launch traced here: 16.7 us
  Pallas kernels  16.1 us (95%)
  between operations  0.64 us (4%)
    pallas_call x1, Pallas kernels, on_device(): pl.pallas_call(functools.partial(kernel, n, state_type), out_shape=(jax.S...  15.2 us
    pallas_call x1, Pallas kernels, on_device(): pl.pallas_call(finish, out_shape=(jax.ShapeDtypeStruct(queries.shape, jnp...  0.84 us

profile of v7, /device:TPU:26, one launch (start us, length us, event | category | flops | bytes accessed | tf_op | source)
XLA Modules:
  0.0 16.7 jit_solution(1474576818815198726)
XLA Ops:
  0.6 15.2 %shard_map.113 = (f32[2,128,512]{2,1,0:T(8,128)S(1)}, f32[2,1,512]{2,1,0:T(1,128)S(1)}, bf16[128,512]{1,0:T(8,128)(2,1)S(1)}) custom-call(bf16[128,1024]{1,0:T(8,128)(2,1)} %q_hbm.1, bf16[128,256]{1,0:T(8,128)(2,1)} %k_hbm.1, bf16[128,256]{1,0:T(8,128)(2,1)} %v_hbm.1, s32[1,8]{1,0:T(1,128)} %pat_hbm.1, bf16[128,512]{1,0:T(8,128)(2,1)} %x_hbm.1, ...), custom_call_target="tpu_custom_call" | custom-call | tf_op jit(solution)/shard_map/pallas_call | solution.py:366
  15.9 0.8 %shard_map.114 = (bf16[128,1024]{1,0:T(8,128)(2,1)}, bf16[128,512]{1,0:T(8,128)(2,1)}) custom-call(f32[2,128,512]{2,1,0:T(8,128)S(1)} %get-tuple-element.5.acc_ref, f32[2,1,512]{2,1,0:T(1,128)S(1)} %get-tuple-element.6.sum_ref, bf16[128,512]{1,0:T(8,128)(2,1)S(1)} %get-tuple-element.7.ssm_ref), custom_call_target="tpu_custom_call" | custom-call | tf_op jit(solution)/shard_map/pallas_call | solution.py:392

commit v8 on v6

--- a/solution.py
+++ b/solution.py
@@ -248,11 +248,11 @@
             y_ref[:, at] = y_ref[:, at] + dot_state(c_ref[...], s_in[k]) * growth
             grow_ref[:, at] = growth * decay_other[:, at]
 
-    @pl.when(pair >= 2)
+    @pl.when(pair >= 3)
     def _():
         own_block()
 
-    @pl.when(pair >= 2)
+    @pl.when(pair >= 3)
     def _():
         earlier_block(1)
 
@@ -281,11 +281,11 @@
     inverse = lax.rsqrt(square / width + 1e-05)
     ssm_ref[...] = (gated * inverse * gain_ref[...]).astype(jnp.bfloat16)
 
-    @pl.when(pair < 2)
+    @pl.when(pair < 3)
     def _():
         own_block()
 
-    @pl.when(pair == 1)
+    @pl.when((pair == 1) | (pair == 2))
     def _():
         earlier_block(1)
 

time: 16.6 us -> 16.6 us (level)
  no operation moved by 1% of the time
where the time goes in v8:
time: 16.6 us; the launch traced here: 16.4 us
  Pallas kernels  15.8 us (95%)
  between operations  0.64 us (4%)
    pallas_call x1, Pallas kernels, on_device(): pl.pallas_call(functools.partial(kernel, n, state_type), out_shape=(jax.S...  14.9 us
    pallas_call x1, Pallas kernels, on_device(): pl.pallas_call(finish, out_shape=(jax.ShapeDtypeStruct(queries.shape, jnp...  0.84 us

profile of v8, /device:TPU:24, one launch (start us, length us, event | category | flops | bytes accessed | tf_op | source)
XLA Modules:
  0.0 16.4 jit_solution(11521564170523029459)
XLA Ops:
  0.6 14.9 %shard_map.113 = (f32[2,128,512]{2,1,0:T(8,128)S(1)}, f32[2,1,512]{2,1,0:T(1,128)S(1)}, bf16[128,512]{1,0:T(8,128)(2,1)S(1)}) custom-call(bf16[128,1024]{1,0:T(8,128)(2,1)} %q_hbm.1, bf16[128,256]{1,0:T(8,128)(2,1)} %k_hbm.1, bf16[128,256]{1,0:T(8,128)(2,1)} %v_hbm.1, s32[1,8]{1,0:T(1,128)} %pat_hbm.1, bf16[128,512]{1,0:T(8,128)(2,1)} %x_hbm.1, ...), custom_call_target="tpu_custom_call" | custom-call | tf_op jit(solution)/shard_map/pallas_call | solution.py:367
  15.6 0.8 %shard_map.114 = (bf16[128,1024]{1,0:T(8,128)(2,1)}, bf16[128,512]{1,0:T(8,128)(2,1)}) custom-call(f32[2,128,512]{2,1,0:T(8,128)S(1)} %get-tuple-element.5.acc_ref, f32[2,1,512]{2,1,0:T(1,128)S(1)} %get-tuple-element.6.sum_ref, bf16[128,512]{1,0:T(8,128)(2,1)S(1)} %get-tuple-element.7.ssm_ref), custom_call_target="tpu_custom_call" | custom-call | tf_op jit(solution)/shard_map/pallas_call | solution.py:393
